TPU v7x, 512 devices: a whole 4x8x8 slice. The times are simulated.
512 devices in a mesh: inst: 64 (over z, x, core), tp: 8 (over y).
Axes of the slice: x: 4, y: 8, z: 8, core: 2. Of those that a mesh axis runs over, the one named last changes fastest.
Arguments:
- queries: bfloat16 [512, 8192], P('inst', 'tp'), may hold values from -4 to 4
- pool_keys: bfloat16 [2048, 128, 1024], P('inst', None, 'tp'), may hold values from -16 to 16
- pool_values: bfloat16 [2048, 128, 1024], P('inst', None, 'tp'), may hold values from -6 to 6
- block_table: int32 [512, 4], P('inst'), may hold values from 0 to 2047, as said below
- ctx_len: int32 [512], P('inst'), may hold values from 1 to 512, 196608 in all
- out_weight: bfloat16 [8192, 8192], P('tp', 'inst'), may hold values from -0.5 to 0.5
Outputs:
- layer_out: bfloat16 [512, 8192], P('tp', 'inst')
Inputs may be any that keep to these rules, and one draw needn't show every extreme that they name: block_table[r, b] is the pool slot of block b of request r (entries past the request's length are still valid slots); every pool slot holds exactly one (request, block) entry of the table; instance i owns slots i * 32 to (i + 1) * 32 - 1 and request r has home instance r // 8. Of the 32 entries of one home's requests, at most 2 lie on any one instance; exactly 2 lie on the instance after the home (counted round), and some lie on the instance before it.
All inputs are finite; a program needn't handle non-finite values. No bound on the sum of `ctx_len` on one device may be relied on, other than what follows from the above.
Results may differ from a plain program's by a relative error of at most 0.005.
Values may be sent and summed in bfloat16 or wider, within the bound.
No kernel may reach another device: no remote copies, remote signals or barrier semaphores. Data moves between devices by JAX's collectives and lax.ppermute only.
A program may use at most 64 MiB of HBM per device.

v0:
```python
import jax
import jax.numpy as jnp
from jax import lax
from jax.sharding import PartitionSpec as P

HD = 128
BLOCK = 128
MAXB = 4


very_low = -1e30


def block_partials(q_items, slot_ids, counts, pool_keys, pool_values):
    count_src, count_slot = slot_ids.shape
    kv_heads = pool_keys.shape[2] // HD
    q_heads = q_items.shape[2] // HD
    per_group = q_heads // kv_heads
    key_rows = pool_keys[slot_ids].reshape(count_src, count_slot, BLOCK, kv_heads, HD)
    value_rows = pool_values[slot_ids].reshape(count_src, count_slot, BLOCK, kv_heads, HD)
    grouped = q_items.reshape(count_src, count_slot, kv_heads, per_group, HD)
    scores = jnp.einsum(
        "nckgd,nctkd->nckgt", grouped, key_rows, preferred_element_type=jnp.float32
    ) * HD ** (-0.5)
    usable = (
        lax.broadcasted_iota(jnp.int32, (1, 1, 1, 1, BLOCK), 4) < counts[:, :, None, None, None]
    )
    scores = jnp.where(usable, scores, very_low)
    maxima = jnp.max(scores, axis=4)
    weights = jnp.where(usable, jnp.exp(scores - maxima[..., None]), 0.0)
    totals = jnp.sum(weights, axis=4)
    output = jnp.einsum(
        "nckgt,nctkd->nckgd",
        weights.astype(jnp.bfloat16),
        value_rows,
        preferred_element_type=jnp.float32,
    )
    return (
        output.reshape(count_src, count_slot, q_heads * HD),
        maxima.reshape(count_src, count_slot, q_heads),
        totals.reshape(count_src, count_slot, q_heads),
    )


def per_device(queries, pool_keys, pool_values, block_table, ctx_len, out_weight):
    instances = lax.axis_size("inst")
    slots_dev = pool_keys.shape[0]
    requests_dev = queries.shape[0]
    q_heads = queries.shape[1] // HD
    slot_cap = max(2, (slots_dev + instances - 1) // instances)
    buffer_len = instances * slot_cap
    flat_slot = block_table.reshape(-1)
    entry = jnp.arange(flat_slot.shape[0], dtype=jnp.int32)
    request = entry // MAXB
    counts = jnp.clip(ctx_len[request] - entry % MAXB * BLOCK, 0, BLOCK)
    is_live = counts > 0
    holder = flat_slot // slots_dev
    hits = (
        (holder[:, None] == jnp.arange(instances, dtype=jnp.int32)[None, :]) & is_live[:, None]
    ).astype(jnp.int32)
    order_in = jnp.sum((jnp.cumsum(hits, axis=0) - hits) * hits, axis=1)
    send_pos = jnp.where(is_live, holder * slot_cap + order_in, buffer_len)
    owner_req = jnp.full((buffer_len,), -1, jnp.int32).at[send_pos].set(request, mode="drop")
    q_send = (
        jnp.zeros((buffer_len, queries.shape[1]), jnp.bfloat16)
        .at[send_pos]
        .set(queries[request], mode="drop")
    )
    slot_meta = (
        jnp.zeros((buffer_len, 2), jnp.int32)
        .at[send_pos]
        .set(jnp.stack([flat_slot % slots_dev, counts], axis=1), mode="drop")
    )
    q_items = lax.all_to_all(
        q_send.reshape(instances, slot_cap, -1), "inst", split_axis=0, concat_axis=0, tiled=True
    )
    meta_items = lax.all_to_all(
        slot_meta.reshape(instances, slot_cap, 2), "inst", split_axis=0, concat_axis=0, tiled=True
    )
    part_out, part_max, part_sum = block_partials(
        q_items, meta_items[..., 0], meta_items[..., 1], pool_keys, pool_values
    )
    back_out = lax.all_to_all(part_out, "inst", split_axis=0, concat_axis=0, tiled=True)
    back_max = lax.all_to_all(part_max, "inst", split_axis=0, concat_axis=0, tiled=True)
    back_sum = lax.all_to_all(part_sum, "inst", split_axis=0, concat_axis=0, tiled=True)
    flat_out = back_out.reshape(buffer_len, q_heads, HD)
    flat_max = back_max.reshape(buffer_len, q_heads)
    flat_sum = back_sum.reshape(buffer_len, q_heads)
    selector = owner_req[None, :] == jnp.arange(requests_dev, dtype=jnp.int32)[:, None]
    req_max = jnp.max(jnp.where(selector[:, :, None], flat_max[None], very_low), axis=1)
    item_max = jnp.max(jnp.where(selector[:, :, None], req_max[:, None, :], very_low), axis=0)
    item_scale = jnp.where((owner_req >= 0)[:, None], jnp.exp(flat_max - item_max), 0.0)
    select_float = selector.astype(jnp.float32)
    totals = jnp.dot(select_float, item_scale * flat_sum, precision=lax.Precision.HIGHEST)
    weighted = (item_scale[:, :, None] * flat_out).reshape(buffer_len, q_heads * HD)
    merged = jnp.dot(select_float, weighted, precision=lax.Precision.HIGHEST)
    attention = (
        (merged.reshape(requests_dev, q_heads, HD) / totals[:, :, None])
        .reshape(requests_dev, q_heads * HD)
        .astype(jnp.bfloat16)
    )
    all_attention = lax.all_gather(attention, "inst", axis=0, tiled=True)
    summed = lax.psum_scatter(
        jnp.dot(all_attention, out_weight, preferred_element_type=jnp.float32),
        "tp",
        scatter_dimension=0,
        tiled=True,
    )
    return summed.astype(jnp.bfloat16)


def solution(mesh):
    in_specs = (
        P("inst", "tp"),
        P("inst", None, "tp"),
        P("inst", None, "tp"),
        P("inst", None),
        P("inst"),
        P("tp", "inst"),
    )
    out_specs = P("tp", "inst")
    return jax.shard_map(
        per_device, mesh=mesh, in_specs=in_specs, out_specs=out_specs, check_vma=False
    )
```

profile of v0, /device:TPU:6, one launch (start us, length us, event | category | flops | bytes accessed | tf_op | source)
XLA Modules:
  0.0 240.0 jit_solution(17243001254098212917)
XLA Ops:
  6.5 0.8 copy.43
  7.6 1.4 gather_fusion
  9.1 0.2 select_reduce_fusion.1
  9.4 0.7 scatter_custom_fusion.1
  10.1 1.1 copy.47
  11.2 13.8 %all-to-all-start = ((s32[64,2,2]{1,2,0:T(2,128)}), s32[64,2,2]{1,2,0:T(2,128)S(1)}, u32[]{:S(2)}, u32[]{:S(2)}) async-start(s32[64,2,2]{1,2,0:T(2,128)} %copy.47), calls=%async_computation | async-start | bytes 131072 | tf_op jit(solution)/shard_map/all_to_all | solution.py:77
  25.0 2.0 scatter_custom_fusion.2
  27.0 0.8 reshape.336
  27.8 5.3 %all-to-all-done = s32[64,2,2]{1,2,0:T(2,128)S(1)} async-done(((s32[64,2,2]{1,2,0:T(2,128)}), s32[64,2,2]{1,2,0:T(2,128)S(1)}, u32[]{:S(2)}, u32[]{:S(2)}) %all-to-all-start) | async-done | bytes 1056 | tf_op jit(solution)/shard_map/all_to_all | solution.py:77
  33.1 6.5 %all-to-all-start.1 = ((bf16[64,2,1024]{2,1,0:T(2,128)(2,1)}), bf16[64,2,1024]{2,1,0:T(2,128)(2,1)S(1)}, u32[]{:S(2)}, u32[]{:S(2)}) async-start(bf16[64,2,1024]{2,1,0:T(2,128)(2,1)} %reshape.336), calls=%async_computation.1 | async-start | bytes 524288 | tf_op jit(solution)/shard_map/all_to_all | solution.py:74
  39.9 3.0 %gather_fusion.1 = bf16[128,128,128]{2,1,0:T(8,128)(2,1)} fusion(bf16[32,128,128]{2,1,0:T(8,128)(2,1)S(1)} %copy-done, s32[1024]{0:T(1024)S(1)} %pad_clamp_fusion), kind=kCustom, calls=%fused_computation.2 | custom fusion | bytes 8389120 | tf_op jit(solution)/shard_map/gather | solution.py:19
  43.0 8.6 %all-to-all-done.1 = bf16[64,2,1024]{2,1,0:T(2,128)(2,1)S(1)} async-done(((bf16[64,2,1024]{2,1,0:T(2,128)(2,1)}), bf16[64,2,1024]{2,1,0:T(2,128)(2,1)S(1)}, u32[]{:S(2)}, u32[]{:S(2)}) %all-to-all-start.1) | async-done | bytes 262176 | tf_op jit(solution)/shard_map/all_to_all | solution.py:74
  51.6 0.2 reshape.337
  51.8 5.2 %fusion.41 = (f32[64,2,8]{2,1,0:T(2,128)}, f32[64,2,8,128]{3,2,1,0:T(8,128)S(1)}) fusion(bf16[64,2,8,128]{3,2,1,0:T(8,128)(2,1)S(1)} %reshape.337, bf16[64,2,128,128]{3,2,1,0:T(8,128)(2,1)} %bitcast.38, pred[64,2,128]{2,1,0:T(4,128)(4,1)S(1)} %iota_compare_fusion), kind=kOutput, calls=%fused_computation.86 | convolution fusion | flops 33946624 | bytes 5001216 | tf_op jit(solution)/shard_map/nckgd,nctkd->nckgt/dot_general | solution.py:22
  57.0 1.9 fusion.5
  58.9 5.9 %all-to-all-start.4 = ((f32[64,2,8]{2,1,0:T(2,128)}), f32[64,2,8]{2,1,0:T(2,128)S(1)}, u32[]{:S(2)}, u32[]{:S(2)}) async-start(f32[64,2,8]{2,1,0:T(2,128)} %fusion.5), calls=%async_computation.4 | async-start | bytes 131072 | tf_op jit(solution)/shard_map/all_to_all | solution.py:85
  64.8 3.0 %gather_fusion.2 = bf16[128,128,128]{2,1,0:T(8,128)(2,1)} fusion(bf16[32,128,128]{2,1,0:T(8,128)(2,1)S(1)} %copy-done.1, s32[1024]{0:T(1024)S(1)} %pad_clamp_fusion), kind=kCustom, calls=%fused_computation.3 | custom fusion | bytes 8389120 | tf_op jit(solution)/shard_map/gather | solution.py:20
  67.8 5.0 %all-to-all-done.4 = f32[64,2,8]{2,1,0:T(2,128)S(1)} async-done(((f32[64,2,8]{2,1,0:T(2,128)}), f32[64,2,8]{2,1,0:T(2,128)S(1)}, u32[]{:S(2)}, u32[]{:S(2)}) %all-to-all-start.4) | async-done | bytes 4128 | tf_op jit(solution)/shard_map/all_to_all | solution.py:85
  72.8 6.5 %all-to-all-start.2 = ((f32[64,2,8]{2,1,0:T(2,128)}), f32[64,2,8]{2,1,0:T(2,128)S(1)}, u32[]{:S(2)}, u32[]{:S(2)}) async-start(f32[64,2,8]{2,1,0:T(2,128)} %get-tuple-element.10), calls=%async_computation.2 | async-start | bytes 131072 | tf_op jit(solution)/shard_map/all_to_all | solution.py:84
  79.3 3.5 %fusion.7 = f32[64,2,8,128]{3,2,1,0:T(8,128)S(1)} fusion(bf16[64,2,128,128]{3,2,1,0:T(8,128)(2,1)} %bitcast.39, f32[64,2,8,128]{3,2,1,0:T(8,128)S(1)} %get-tuple-element.11, f32[64,2,8]{2,1,0:T(2,128)} %get-tuple-element.10, pred[64,2,128]{2,1,0:T(4,128)(4,1)S(1)} %iota_compare_fusion), kind=kOutput, calls=%fused_computation.18 | convolution fusion | flops 33947648 | bytes 5263360 | tf_op jit(solution)/shard_map/nckgt,nctkd->nckgd/dot_general | solution.py:32
  82.8 1.1 reshape.339
  83.9 3.6 %all-to-all-done.2 = f32[64,2,8]{2,1,0:T(2,128)S(1)} async-done(((f32[64,2,8]{2,1,0:T(2,128)}), f32[64,2,8]{2,1,0:T(2,128)S(1)}, u32[]{:S(2)}, u32[]{:S(2)}) %all-to-all-start.2) | async-done | bytes 4128 | tf_op jit(solution)/shard_map/all_to_all | solution.py:84
  87.5 6.8 %all-to-all-start.3 = ((f32[64,2,1024]{2,1,0:T(2,128)}), f32[64,2,1024]{2,1,0:T(2,128)S(1)}, u32[]{:S(2)}, u32[]{:S(2)}) async-start(f32[64,2,1024]{2,1,0:T(2,128)} %reshape.339), calls=%async_computation.3 | async-start | bytes 1048576 | tf_op jit(solution)/shard_map/all_to_all | solution.py:83
  94.3 0.7 scatter_custom_fusion
  95.4 16.4 %all-to-all-done.3 = f32[64,2,1024]{2,1,0:T(2,128)S(1)} async-done(((f32[64,2,1024]{2,1,0:T(2,128)}), f32[64,2,1024]{2,1,0:T(2,128)S(1)}, u32[]{:S(2)}, u32[]{:S(2)}) %all-to-all-start.3) | async-done | bytes 524320 | tf_op jit(solution)/shard_map/all_to_all | solution.py:83
  111.8 0.4 reshape.340
  112.2 0.2 copy.52
  112.5 1.0 fusion.4
  113.5 78.4 %all-gather.2.cloned.1.call-done = bf16[512,1024]{1,0:T(8,128)(2,1)} async-done(((bf16[8,1024]{1,0:T(8,128)(2,1)}), bf16[512,1024]{1,0:T(8,128)(2,1)}) %all-gather.2.cloned.1.call-update) | async-done | bytes 1048592 | tf_op jit(solution)/shard_map/all_gather | solution.py:102
  191.9 2.4 fusion.43
  194.3 37.5 %reduce-scatter.2.cloned.1.call-done = f32[64,128]{1,0:T(8,128)} async-done(((f32[512,128]{1,0:T(8,128)}), f32[64,128]{1,0:T(8,128)}) %reduce-scatter.2.cloned.1.call-update) | async-done | bytes 32784 | tf_op jit(solution)/shard_map/reduce_scatter | solution.py:103
  231.8 1.4 convert_element_type.21
  (34 shorter events, 1.4 us)
Async XLA Ops:
  6.5 33.3 %copy-start = (bf16[32,128,128]{2,1,0:T(8,128)(2,1)S(1)}, bf16[32,128,128]{2,1,0:T(8,128)(2,1)}, u32[]{:S(2)}) copy-start(bf16[32,128,128]{2,1,0:T(8,128)(2,1)} %param.7) | copy-start | bytes 3145732
  11.2 21.9 %all-to-all-start = ((s32[64,2,2]{1,2,0:T(2,128)}), s32[64,2,2]{1,2,0:T(2,128)S(1)}, u32[]{:S(2)}, u32[]{:S(2)}) async-start(s32[64,2,2]{1,2,0:T(2,128)} %copy.47), calls=%async_computation | async-start | bytes 131072 | tf_op jit(solution)/shard_map/all_to_all | solution.py:77
  33.1 18.6 %all-to-all-start.1 = ((bf16[64,2,1024]{2,1,0:T(2,128)(2,1)}), bf16[64,2,1024]{2,1,0:T(2,128)(2,1)S(1)}, u32[]{:S(2)}, u32[]{:S(2)}) async-start(bf16[64,2,1024]{2,1,0:T(2,128)(2,1)} %reshape.336), calls=%async_computation.1 | async-start | bytes 524288 | tf_op jit(solution)/shard_map/all_to_all | solution.py:74
  42.9 21.9 %copy-start.1 = (bf16[32,128,128]{2,1,0:T(8,128)(2,1)S(1)}, bf16[32,128,128]{2,1,0:T(8,128)(2,1)}, u32[]{:S(2)}) copy-start(bf16[32,128,128]{2,1,0:T(8,128)(2,1)} %param.8) | copy-start | bytes 3145732
  58.9 14.0 %all-to-all-start.4 = ((f32[64,2,8]{2,1,0:T(2,128)}), f32[64,2,8]{2,1,0:T(2,128)S(1)}, u32[]{:S(2)}, u32[]{:S(2)}) async-start(f32[64,2,8]{2,1,0:T(2,128)} %fusion.5), calls=%async_computation.4 | async-start | bytes 131072 | tf_op jit(solution)/shard_map/all_to_all | solution.py:85
  72.8 14.7 %all-to-all-start.2 = ((f32[64,2,8]{2,1,0:T(2,128)}), f32[64,2,8]{2,1,0:T(2,128)S(1)}, u32[]{:S(2)}, u32[]{:S(2)}) async-start(f32[64,2,8]{2,1,0:T(2,128)} %get-tuple-element.10), calls=%async_computation.2 | async-start | bytes 131072 | tf_op jit(solution)/shard_map/all_to_all | solution.py:84
  82.8 109.1 %copy-start.2 = (bf16[1024,128]{1,0:T(8,128)(2,1)S(1)}, bf16[1024,128]{1,0:T(8,128)(2,1)}, u32[]{:S(2)}) copy-start(bf16[1024,128]{1,0:T(8,128)(2,1)} %param.11) | copy-start | bytes 786436
  87.5 24.4 %all-to-all-start.3 = ((f32[64,2,1024]{2,1,0:T(2,128)}), f32[64,2,1024]{2,1,0:T(2,128)S(1)}, u32[]{:S(2)}, u32[]{:S(2)}) async-start(f32[64,2,1024]{2,1,0:T(2,128)} %reshape.339), calls=%async_computation.3 | async-start | bytes 1048576 | tf_op jit(solution)/shard_map/all_to_all | solution.py:83
  94.3 97.6 %all-gather.2.cloned.1.call-start = ((), (), s32[]{:S(2)}) async-start(), calls=%async_computation.6 | async-start | bytes 1064960 | tf_op jit(solution)/shard_map/all_gather | solution.py:102
  113.4 118.4 %reduce-scatter.2.cloned.1.call-start = ((), (), s32[]{:S(2)}) async-start(), calls=%async_computation.7 | async-start | bytes 294912 | tf_op jit(solution)/shard_map/reduce_scatter | solution.py:103
Sparse Core Ops, SparseCore 0:
  113.6 78.2 all-gather.1
  194.7 37.1 reduce-scatter.1
where the time goes:
time: 241 us; the launch traced here: 240 us
  waiting for transfers between devices  155 us (64%)
  starting transfers between devices  39.6 us (16%)
  local copies, waits for them, and re-layouts  15.7 us (7%)
  between operations  13.6 us (6%)
  matrix products  12.2 us (5%)
  other arithmetic  4.04 us (2%)
    all_gather x1, waiting for transfers between devices, per_device(): all_attention = lax.all_gather(attention, 'inst', axis=0, tiled=True)  78.4 us
    reduce_scatter x1, waiting for transfers between devices, per_device(): lax.psum_scatter(jnp.dot(all_attention, out_weight, preferred_element_typ...  37.5 us
    all_to_all x1, waiting for transfers between devices, per_device(): lax.all_to_all(part_out, 'inst', split_axis=0, concat_axis=0, tiled=True)  16.4 us
    all_to_all x1, starting transfers between devices, per_device(): lax.all_to_all(slot_meta.reshape(instances, slot_cap, 2), 'inst', split_a...  13.8 us
    all_to_all x1, waiting for transfers between devices, per_device(): lax.all_to_all(q_send.reshape(instances, slot_cap, -1), 'inst', split_axi...  8.59 us
    all_to_all x1, starting transfers between devices, per_device(): lax.all_to_all(part_out, 'inst', split_axis=0, concat_axis=0, tiled=True)  6.77 us
    all_to_all x1, starting transfers between devices, per_device(): lax.all_to_all(q_send.reshape(instances, slot_cap, -1), 'inst', split_axi...  6.53 us
    all_to_all x1, starting transfers between devices, per_device(): lax.all_to_all(part_max, 'inst', split_axis=0, concat_axis=0, tiled=True)  6.5 us
  transfers between devices with their start and end apart: 7, of which 7 were waited for; matrix products, arithmetic and copies ran while one was open for 6% of the time, Pallas kernels for 0%

commit v1 on v0

v1 whole, which is shorter than its diff:
```python
import jax
import jax.numpy as jnp
from jax import lax
from jax.experimental import pallas as pl
from jax.experimental.pallas import tpu as pltpu
from jax.sharding import Mesh, PartitionSpec as P

HD = 128
BLOCK = 128
MAXB = 4
SLOTS = 32
HEADS = 8
REQS = 8
PEERS = 64
MSG = 24
very_low = -1e30
f32 = jnp.float32
bf16 = jnp.bfloat16

VMEM = pl.BlockSpec(memory_space=pltpu.VMEM)
SMEM = pl.BlockSpec(memory_space=pltpu.SMEM)


def route_kernel(table, ctx, q, out, where_to, buf, rows, used):
    buf[...] = jnp.zeros_like(buf)
    for p in range(PEERS):
        used[p] = 0
    whole = q[...].astype(f32)
    for h in range(HEADS):
        rows[pl.ds(h, REQS, stride=HEADS), :] = whole[:, h * HD : (h + 1) * HD]
    lane = lax.broadcasted_iota(jnp.int32, (HEADS, HD), 1)
    for e in range(REQS * MAXB):
        r, b = e // MAXB, e % MAXB
        slot = table[r, b]
        p = slot >> 5
        pos = used[p]
        used[p] = pos + 1
        count = jnp.clip(ctx[r] - b * BLOCK, 0, BLOCK)
        where_to[e] = p * 2 + pos
        buf[pl.ds(pl.multiple_of(p * MSG + pos * 8, 8), 8), :] = rows[r * 8 : r * 8 + 8, :]
        meta = pl.ds(pl.multiple_of(p * MSG + 16, 8), 8)
        note = jnp.where(lane == 2 * pos, (slot & 31) + 1, jnp.where(lane == 2 * pos + 1, count, 0))
        buf[meta, :] = buf[meta, :] + note.astype(f32)
    out[...] = buf[...].astype(bf16)


def attend_kernel(items, keys, values, out):
    got = items[...].astype(f32).reshape(PEERS, 3, 8, HD)
    meta = got[:, 2]
    lane = lax.broadcasted_iota(jnp.int32, (PEERS, 8, SLOTS * HEADS), 2)
    head = lax.broadcasted_iota(jnp.int32, (PEERS, 8, SLOTS * HEADS), 1)
    same_head = (lane & 7) == head
    slot_no = ((lane >> 3) + 1).astype(f32)
    picks, sides = [], []
    for pos in range(2):
        slot = meta[:, :, 2 * pos : 2 * pos + 1]
        count = meta[:, :, 2 * pos + 1 : 2 * pos + 2]
        pick = jnp.where(same_head & (slot_no == slot), 1.0, 0.0)
        picks.append(pick.reshape(PEERS * 8, SLOTS * HEADS).astype(bf16))
        counts = jnp.broadcast_to(count, (PEERS, 8, HD)).reshape(PEERS * 8, HD)
        sides.append(
            jnp.concatenate([got[:, pos].reshape(PEERS * 8, HD), counts], axis=1).astype(bf16)
        )
    by_slot = lax.dot_general(
        jnp.concatenate(picks, axis=0),
        jnp.concatenate(sides, axis=0),
        (((0,), (0,)), ((), ())),
        preferred_element_type=f32,
    )
    query, counts = by_slot[:, :HD], by_slot[:, HD:]
    parts = []
    for s in range(0, SLOTS, 2):
        pair = lax.dot_general(
            query[s * 8 : s * 8 + 16].astype(bf16),
            keys[s : s + 2].reshape(2 * BLOCK, HD),
            (((1,), (1,)), ((), ())),
            preferred_element_type=f32,
        )
        parts += [pair[:8, :BLOCK], pair[8:, BLOCK:]]
    scores = jnp.concatenate(parts, axis=0) * HD ** (-0.5)
    token = lax.broadcasted_iota(jnp.int32, scores.shape, 1).astype(f32)
    usable = token < counts
    scores = jnp.where(usable, scores, very_low)
    top = jnp.max(scores, axis=1, keepdims=True)
    weights = jnp.where(usable, jnp.exp(scores - top), 0.0)
    total = jnp.sum(weights, axis=1, keepdims=True)
    none = jnp.zeros((8, BLOCK), f32)
    parts = []
    for s in range(0, SLOTS, 2):
        first = jnp.concatenate([weights[s * 8 : s * 8 + 8], none], axis=1)
        second = jnp.concatenate([none, weights[s * 8 + 8 : s * 8 + 16]], axis=1)
        parts.append(
            jnp.dot(
                jnp.concatenate([first, second], axis=0).astype(bf16),
                values[s : s + 2].reshape(2 * BLOCK, HD),
                preferred_element_type=f32,
            )
        )
    output = jnp.concatenate(parts, axis=0)
    alive = total > 0.0
    safe = jnp.where(alive, total, 1.0)
    output = (output / safe).astype(bf16)
    lse = jnp.where(alive, top + jnp.log(safe), very_low)
    high = lse.astype(bf16).astype(f32)
    mid = (lse - high).astype(bf16).astype(f32)
    low = lse - high - mid
    at = lax.broadcasted_iota(jnp.int32, (SLOTS * HEADS, HD), 1)
    back = []
    for pos in range(2):
        note = jnp.where(
            at == 3 * pos,
            high,
            jnp.where(at == 3 * pos + 1, mid, jnp.where(at == 3 * pos + 2, low, 0.0)),
        )
        side = jnp.concatenate([output, note.astype(bf16)], axis=1)
        back.append(jnp.dot(picks[pos], side, preferred_element_type=f32))
    notes = back[0][:, HD:] + back[1][:, HD:]
    tiles = [v.reshape(PEERS, 1, 8, HD) for v in (back[0][:, :HD], back[1][:, :HD], notes)]
    out[...] = jnp.concatenate(tiles, axis=1).reshape(PEERS * MSG, HD).astype(bf16)


def merge_kernel(where_to, items, out, got, rows):
    got[...] = items[...].astype(f32)
    lane = lax.broadcasted_iota(jnp.int32, (HEADS, HD), 1)
    for r in range(REQS):
        outs, lses = [], []
        for b in range(MAXB):
            item = where_to[r * MAXB + b]
            p, pos = item >> 1, item & 1
            outs.append(got[pl.ds(pl.multiple_of(p * MSG + pos * 8, 8), 8), :])
            note = got[pl.ds(pl.multiple_of(p * MSG + 16, 8), 8), :]
            mine = (lane >= 3 * pos) & (lane < 3 * pos + 3)
            lses.append(jnp.sum(jnp.where(mine, note, 0.0), axis=1, keepdims=True))
        top = jnp.maximum(jnp.maximum(lses[0], lses[1]), jnp.maximum(lses[2], lses[3]))
        scales = [jnp.exp(v - top) for v in lses]
        total = scales[0] + scales[1] + scales[2] + scales[3]
        merged = sum(s * o for s, o in zip(scales, outs))
        rows[r * 8 : r * 8 + 8, :] = merged / total
    whole = jnp.concatenate(
        [rows[pl.ds(h, REQS, stride=HEADS), :] for h in range(HEADS)], axis=1
    )
    out[...] = jnp.concatenate([whole] * 8, axis=0).astype(bf16)


def project_kernel(attention, weight, out):
    left = attention[...]
    for n in range(8):
        part = jnp.dot(left, weight[n], preferred_element_type=f32)
        out[n * 64 : (n + 1) * 64, :] = part.astype(bf16)


def total_kernel(parts, out):
    got = parts[...].astype(f32).reshape(8, 8, 8, HD)
    out[...] = jnp.sum(got, axis=1).reshape(64, HD).astype(bf16)


def per_device(queries, pool_keys, pool_values, block_table, ctx_len, out_weight):
    inst = ("z", "x", "c")
    limit = pltpu.CompilerParams(vmem_limit_bytes=24 * 1024 * 1024)
    weights = lax.all_gather(out_weight, ("x", "c"), axis=0, tiled=False)
    send, where_to = pl.pallas_call(
        route_kernel,
        out_shape=(
            jax.ShapeDtypeStruct((PEERS * MSG, HD), bf16),
            jax.ShapeDtypeStruct((REQS * MAXB,), jnp.int32),
        ),
        in_specs=[SMEM, SMEM, VMEM],
        out_specs=(VMEM, SMEM),
        scratch_shapes=[
            pltpu.VMEM((PEERS * MSG, HD), f32),
            pltpu.VMEM((REQS * HEADS, HD), f32),
            pltpu.SMEM((PEERS,), jnp.int32),
        ],
        compiler_params=limit,
        name="route",
    )(block_table, ctx_len, queries)
    items = lax.all_to_all(
        send.reshape(PEERS, MSG, HD), inst, split_axis=0, concat_axis=0, tiled=True
    )
    back = pl.pallas_call(
        attend_kernel,
        out_shape=jax.ShapeDtypeStruct((PEERS * MSG, HD), bf16),
        in_specs=[VMEM, VMEM, VMEM],
        out_specs=VMEM,
        compiler_params=limit,
        name="attend",
    )(items.reshape(PEERS * MSG, HD), pool_keys, pool_values)
    partials = lax.all_to_all(
        back.reshape(PEERS, MSG, HD), inst, split_axis=0, concat_axis=0, tiled=True
    )
    attention = pl.pallas_call(
        merge_kernel,
        out_shape=jax.ShapeDtypeStruct((8 * REQS, HEADS * HD), bf16),
        in_specs=[SMEM, VMEM],
        out_specs=VMEM,
        scratch_shapes=[
            pltpu.VMEM((PEERS * MSG, HD), f32),
            pltpu.VMEM((REQS * HEADS, HD), f32),
        ],
        compiler_params=limit,
        name="merge",
    )(where_to, partials.reshape(PEERS * MSG, HD))
    gathered = lax.all_to_all(
        attention.reshape(8, REQS, HEADS * HD), "z", split_axis=0, concat_axis=0, tiled=True
    )
    parts = pl.pallas_call(
        project_kernel,
        out_shape=jax.ShapeDtypeStruct((512, HD), bf16),
        in_specs=[VMEM, VMEM],
        out_specs=VMEM,
        compiler_params=limit,
        name="project",
    )(gathered.reshape(64, HEADS * HD), weights)
    swapped = lax.all_to_all(
        parts.reshape(64, 8, HD), ("x", "c", "tp"), split_axis=0, concat_axis=0, tiled=True
    )
    return pl.pallas_call(
        total_kernel,
        out_shape=jax.ShapeDtypeStruct((64, HD), bf16),
        in_specs=[VMEM],
        out_specs=VMEM,
        name="total",
    )(swapped.reshape(512, HD))


def solution(mesh):
    split = Mesh(mesh.devices.reshape(8, 4, 2, 8), ("z", "x", "c", "tp"))
    inst = ("z", "x", "c")
    in_specs = (
        P(inst, "tp"),
        P(inst, None, "tp"),
        P(inst, None, "tp"),
        P(inst, None),
        P(inst),
        P("tp", inst),
    )
    return jax.shard_map(
        per_device, mesh=split, in_specs=in_specs, out_specs=P("tp", inst), check_vma=False
    )
```

time: 241 us -> 109 us (0.45)
  the two profiles are of different devices: /device:TPU:6 before, /device:TPU:1 now
where the time goes in v1:
time: 109 us; the launch traced here: 108 us
  blocking collectives  81.9 us (75%)
  between operations  13.4 us (12%)
  local copies, waits for them, and re-layouts  6.21 us (6%)
  Pallas kernels  5.83 us (5%)
    all_to_all x1, blocking collectives, per_device(): lax.all_to_all(send.reshape(PEERS, MSG, HD), inst, split_axis=0, concat_a...  29.8 us
    all_to_all x1, blocking collectives, per_device(): lax.all_to_all(parts.reshape(64, 8, HD), ('x', 'c', 'tp'), split_axis=0,...  20.7 us
    all_to_all x1, blocking collectives, per_device(): lax.all_to_all(back.reshape(PEERS, MSG, HD), inst, split_axis=0, concat_a...  20.4 us
    all_to_all x1, blocking collectives, per_device(): lax.all_to_all(attention.reshape(8, REQS, HEADS * HD), 'z', split_axis=0,...  10.9 us
    unnamed x11, local copies, waits for them, and re-layouts  6.21 us
  transfers between devices with their start and end apart: 1, of which 0 were waited for; matrix products, arithmetic and copies ran while one was open for 1% of the time, Pallas kernels for 4%

profile of v1, /device:TPU:1, one launch (start us, length us, event | category | flops | bytes accessed | tf_op | source)
XLA Modules:
  0.0 108.1 jit_solution(4001165309760097965)
XLA Ops:
  6.5 0.0 all-gather.3.cloned.1.call-start
  6.5 0.7 all-gather.3.cloned.1.call-update
  7.3 0.8 copy.7.table
  8.0 0.0 copy-start.3
  8.0 0.7 copy-done.3
  8.7 0.0 copy-start.4
  8.7 0.7 copy-done.4
  9.4 1.4 %route.1 = (bf16[1536,128]{1,0:T(8,128)(2,1)S(1)}, s32[32]{0:T(128)S(1)}) custom-call(s32[8,4]{1,0:T(8,128)S(1)} %copy.7.table, s32[8]{0:T(128)S(1)} %copy-done.4, bf16[8,1024]{1,0:T(8,128)(2,1)S(1)} %copy-done.3), custom_call_target="tpu_custom_call" | custom-call | tf_op jit(solution)/shard_map/route/pallas_call | solution.py:161
  10.8 29.8 %all_to_all.20 = bf16[64,24,128]{2,1,0:T(8,128)(2,1)S(1)} all-to-all(bf16[64,24,128]{2,1,0:T(8,128)(2,1)S(1)} %bitcast.16), channel_id=1, replica_groups=mesh['z'=8,'x'=4,'c'=2,'tp'=8] {'z','x','c'}, dimensions={0} | all-to-all | bytes 786432 | tf_op jit(solution)/shard_map/all_to_all | solution.py:177
  40.6 0.0 copy-start.1
  40.6 1.2 %copy-done.1 = bf16[32,128,128]{2,1,0:T(8,128)(2,1)S(1)} copy-done((bf16[32,128,128]{2,1,0:T(8,128)(2,1)S(1)}, bf16[32,128,128]{2,1,0:T(8,128)(2,1)}, u32[]{:S(2)}) %copy-start.1) | copy-done | bytes 1048600
  41.8 0.0 copy-start.2
  41.8 1.3 %copy-done.2 = bf16[32,128,128]{2,1,0:T(8,128)(2,1)S(1)} copy-done((bf16[32,128,128]{2,1,0:T(8,128)(2,1)S(1)}, bf16[32,128,128]{2,1,0:T(8,128)(2,1)}, u32[]{:S(2)}) %copy-start.2) | copy-done | bytes 1048600
  43.1 1.7 %attend.1 = bf16[1536,128]{1,0:T(8,128)(2,1)S(1)} custom-call(bf16[1536,128]{1,0:T(8,128)(2,1)S(1)} %bitcast.11, bf16[32,128,128]{2,1,0:T(8,128)(2,1)S(1)} %copy-done.1, bf16[32,128,128]{2,1,0:T(8,128)(2,1)S(1)} %copy-done.2), custom_call_target="tpu_custom_call" | custom-call | tf_op jit(solution)/shard_map/attend/pallas_call | solution.py:180
  44.8 20.4 %all_to_all.21 = bf16[64,24,128]{2,1,0:T(8,128)(2,1)S(1)} all-to-all(bf16[64,24,128]{2,1,0:T(8,128)(2,1)S(1)} %bitcast.12), channel_id=1, replica_groups=mesh['z'=8,'x'=4,'c'=2,'tp'=8] {'z','x','c'}, dimensions={0} | all-to-all | bytes 786432 | tf_op jit(solution)/shard_map/all_to_all | solution.py:188
  65.2 0.8 merge.1
  66.0 10.9 %all_to_all.22 = bf16[8,8,1024]{2,1,0:T(8,128)(2,1)S(1)} all-to-all(bf16[8,8,1024]{2,1,0:T(8,128)(2,1)S(1)} %bitcast.14), channel_id=1, replica_groups=mesh['z'=8,'x'=4,'c'=2,'tp'=8] {'z'}, dimensions={0} | all-to-all | bytes 262144 | tf_op jit(solution)/shard_map/all_to_all | solution.py:203
  76.9 0.0 all-gather.3.cloned.1.call-done
  76.9 0.0 copy-start
  76.9 1.6 %copy-done = bf16[8192,128]{1,0:T(8,128)(2,1)S(1)} copy-done((bf16[8192,128]{1,0:T(8,128)(2,1)S(1)}, bf16[8192,128]{1,0:T(8,128)(2,1)}, u32[]{:S(2)}) %copy-start) | copy-done | bytes 2097176
  78.5 0.4 project.1
  79.0 20.7 %all_to_all.23 = bf16[64,8,128]{2,1,0:T(8,128)(2,1)} all-to-all(bf16[64,8,128]{2,1,0:T(8,128)(2,1)S(1)} %bitcast.15), channel_id=1, replica_groups=mesh['z'=8,'x'=4,'c'=2,'tp'=8] {'x','c','tp'}, dimensions={0} | all-to-all | bytes 262144 | tf_op jit(solution)/shard_map/all_to_all | solution.py:214
  99.7 1.5 %total.1 = bf16[64,128]{1,0:T(8,128)(2,1)} custom-call(bf16[512,128]{1,0:T(8,128)(2,1)} %bitcast.17), custom_call_target="tpu_custom_call" | custom-call | tf_op jit(solution)/shard_map/total/pallas_call | solution.py:217
Async XLA Ops:
  6.5 70.4 %all-gather.3.cloned.1.call-start = ((), (), s32[]{:S(2)}) async-start(), calls=%async_computation.4 | async-start | bytes 2359296 | tf_op jit(solution)/shard_map/all_gather | solution.py:160
  8.0 0.7 copy-start.3
  8.7 0.7 copy-start.4
  40.6 1.2 %copy-start.1 = (bf16[32,128,128]{2,1,0:T(8,128)(2,1)S(1)}, bf16[32,128,128]{2,1,0:T(8,128)(2,1)}, u32[]{:S(2)}) copy-start(bf16[32,128,128]{2,1,0:T(8,128)(2,1)} %keys.1) | copy-start | bytes 3145732
  41.8 1.3 %copy-start.2 = (bf16[32,128,128]{2,1,0:T(8,128)(2,1)S(1)}, bf16[32,128,128]{2,1,0:T(8,128)(2,1)}, u32[]{:S(2)}) copy-start(bf16[32,128,128]{2,1,0:T(8,128)(2,1)} %values.1) | copy-start | bytes 3145732
  76.9 1.6 %copy-start = (bf16[8192,128]{1,0:T(8,128)(2,1)S(1)}, bf16[8192,128]{1,0:T(8,128)(2,1)}, u32[]{:S(2)}) copy-start(bf16[8192,128]{1,0:T(8,128)(2,1)} %all-gather.3.cloned.1.call-done) | copy-start | bytes 6291460
Sparse Core Ops, SparseCore 0:
  9.5 37.9 all-gather.2

commit v2 on v1

v2 whole, which is shorter than its diff:
```python
import jax
import jax.numpy as jnp
from jax import lax
from jax.experimental import pallas as pl
from jax.experimental.pallas import tpu as pltpu
from jax.sharding import Mesh, PartitionSpec as P

HD = 128
BLOCK = 128
MAXB = 4
SLOTS = 32
HEADS = 8
REQS = 8
PEERS = 64
MSG = 18
very_low = -1e30
f32 = jnp.float32
bf16 = jnp.bfloat16

VMEM = pl.BlockSpec(memory_space=pltpu.VMEM)
SMEM = pl.BlockSpec(memory_space=pltpu.SMEM)
HBM = pl.BlockSpec(memory_space=pltpu.HBM)
limit = pltpu.CompilerParams(vmem_limit_bytes=24 * 1024 * 1024)


def route_kernel(table_in, ctx_in, q_in, out, where_to, table, ctx, q, buf, rows, used, sems):
    copies = [
        pltpu.make_async_copy(src, dst, sems.at[n])
        for n, (src, dst) in enumerate(((table_in, table), (ctx_in, ctx), (q_in, q)))
    ]
    for copy in copies:
        copy.start()
    buf[...] = jnp.zeros_like(buf)
    for p in range(PEERS):
        used[p] = 0
    for copy in copies:
        copy.wait()
    whole = q[...].astype(f32)
    for h in range(HEADS):
        rows[pl.ds(h, REQS, stride=HEADS), :] = whole[:, h * HD : (h + 1) * HD]
    lane = lax.broadcasted_iota(jnp.int32, (1, HD), 1)
    for e in range(REQS * MAXB):
        r, b = e // MAXB, e % MAXB
        slot = table[b, r]
        p = slot >> 5
        pos = used[p]
        used[p] = pos + 1
        count = jnp.clip(ctx[r] - b * BLOCK, 0, BLOCK)
        first = p * MSG + pos
        where_to[e] = first
        buf[pl.ds(first, HEADS, stride=2), :] = rows[r * 8 : r * 8 + 8, :]
        note = jnp.where(lane == 0, (slot & 31) + 1, jnp.where(lane == 1, count, 0))
        buf[pl.ds(first + 16, 1), :] = note.astype(f32)
    out[...] = buf[...].astype(bf16)


def attend_kernel(items, keys, values, out, buf, rows, counts):
    buf[...] = items[...].astype(f32)
    notes = jnp.concatenate([buf[pl.ds(16 + i, PEERS, stride=MSG), :] for i in range(2)], axis=0)
    queries = jnp.concatenate(
        [
            jnp.concatenate(
                [buf[pl.ds(2 * h + i, PEERS, stride=MSG), :] for h in range(HEADS)], axis=1
            )
            for i in range(2)
        ],
        axis=0,
    )
    slot_no = lax.broadcasted_iota(jnp.int32, (2 * PEERS, HD), 1).astype(f32) + 1.0
    pick = jnp.where(slot_no == notes[:, :1], 1.0, 0.0).astype(bf16)
    side = jnp.concatenate(
        [queries, jnp.broadcast_to(notes[:, 1:2], (2 * PEERS, HD))], axis=1
    ).astype(bf16)
    by_slot = lax.dot_general(
        pick, side, (((0,), (0,)), ((), ())), preferred_element_type=f32
    )[:SLOTS]
    for h in range(HEADS):
        rows[pl.ds(h, SLOTS, stride=HEADS), :] = by_slot[:, h * HD : (h + 1) * HD]
        counts[pl.ds(h, SLOTS, stride=HEADS), :] = by_slot[:, HEADS * HD :]
    parts = []
    for s in range(0, SLOTS, 2):
        pair = lax.dot_general(
            rows[s * 8 : s * 8 + 16, :].astype(bf16),
            keys[s : s + 2].reshape(2 * BLOCK, HD),
            (((1,), (1,)), ((), ())),
            preferred_element_type=f32,
        )
        parts += [pair[:8, :BLOCK], pair[8:, BLOCK:]]
    scores = jnp.concatenate(parts, axis=0) * HD ** (-0.5)
    token = lax.broadcasted_iota(jnp.int32, scores.shape, 1).astype(f32)
    usable = token < counts[...]
    scores = jnp.where(usable, scores, very_low)
    top = jnp.max(scores, axis=1, keepdims=True)
    weights = jnp.where(usable, jnp.exp(scores - top), 0.0)
    total = jnp.sum(weights, axis=1, keepdims=True)
    none = jnp.zeros((8, BLOCK), f32)
    parts = []
    for s in range(0, SLOTS, 2):
        first = jnp.concatenate([weights[s * 8 : s * 8 + 8], none], axis=1)
        second = jnp.concatenate([none, weights[s * 8 + 8 : s * 8 + 16]], axis=1)
        parts.append(
            jnp.dot(
                jnp.concatenate([first, second], axis=0).astype(bf16),
                values[s : s + 2].reshape(2 * BLOCK, HD),
                preferred_element_type=f32,
            )
        )
    alive = total > 0.0
    safe = jnp.where(alive, total, 1.0)
    rows[...] = jnp.concatenate(parts, axis=0) / safe
    lse = jnp.where(alive, top + jnp.log(safe), very_low)
    high = lse.astype(bf16).astype(f32)
    mid = (lse - high).astype(bf16).astype(f32)
    low = lse - high - mid
    lane = lax.broadcasted_iota(jnp.int32, (SLOTS * HEADS, HD), 1)
    head = lax.broadcasted_iota(jnp.int32, (SLOTS * HEADS, HD), 0) & 7
    note = jnp.where(
        lane == head,
        high,
        jnp.where(lane == head + 8, mid, jnp.where(lane == head + 16, low, 0.0)),
    )
    note = jnp.sum(note.reshape(SLOTS, HEADS, HD), axis=1)
    side = jnp.concatenate(
        [rows[pl.ds(h, SLOTS, stride=HEADS), :] for h in range(HEADS)] + [note], axis=1
    ).astype(bf16)
    back = jnp.dot(pick[:, :SLOTS], side, preferred_element_type=f32)
    for i in range(2):
        for j in range(HEADS + 1):
            buf[pl.ds(2 * j + i, PEERS, stride=MSG), :] = back[
                i * PEERS : (i + 1) * PEERS, j * HD : (j + 1) * HD
            ]
    out[...] = buf[...].astype(bf16)


def merge_kernel(where_to, items, out, got, rows):
    got[...] = items[...].astype(f32)
    lane = lax.broadcasted_iota(jnp.int32, (HEADS, HD), 1)
    head = lax.broadcasted_iota(jnp.int32, (HEADS, HD), 0)
    mine = ((lane & 7) == head) & (lane < 24)
    for r in range(REQS):
        outs, lses = [], []
        for b in range(MAXB):
            first = where_to[r * MAXB + b]
            outs.append(got[pl.ds(first, HEADS, stride=2), :])
            note = jnp.broadcast_to(got[pl.ds(first + 16, 1), :], (HEADS, HD))
            lses.append(jnp.sum(jnp.where(mine, note, 0.0), axis=1, keepdims=True))
        top = jnp.maximum(jnp.maximum(lses[0], lses[1]), jnp.maximum(lses[2], lses[3]))
        scales = [jnp.exp(v - top) for v in lses]
        total = scales[0] + scales[1] + scales[2] + scales[3]
        merged = sum(s * o for s, o in zip(scales, outs))
        rows[r * 8 : r * 8 + 8, :] = merged / total
    whole = jnp.concatenate(
        [rows[pl.ds(h, REQS, stride=HEADS), :] for h in range(HEADS)], axis=1
    )
    out[...] = jnp.concatenate([whole] * 8, axis=0).astype(bf16)


def stage_kernel(*refs):
    n = (len(refs) - 1) // 2
    sources, targets, sems = refs[:n], refs[n : 2 * n], refs[-1]
    copies = []
    for a in range(n):
        step = sources[a].shape[0] // 4
        for k in range(4):
            part = pl.ds(k * step, step)
            copies.append(
                pltpu.make_async_copy(sources[a].at[part], targets[a].at[part], sems.at[a * 4 + k])
            )
    for copy in copies:
        copy.start()
    for copy in copies:
        copy.wait()


def stage(*arrays, name):
    return pl.pallas_call(
        stage_kernel,
        out_shape=tuple(jax.ShapeDtypeStruct(a.shape, a.dtype) for a in arrays),
        in_specs=[HBM] * len(arrays),
        out_specs=(VMEM,) * len(arrays),
        scratch_shapes=[pltpu.SemaphoreType.DMA((4 * len(arrays),))],
        compiler_params=limit,
        cost_estimate=pl.CostEstimate(flops=0, bytes_accessed=1 << 22, transcendentals=0),
        name=name,
    )(*arrays)


def project_kernel(attention, weight, out):
    left = attention[...]
    for n in range(8):
        part = jnp.dot(left, weight[n], preferred_element_type=f32)
        out[n * 64 : (n + 1) * 64, :] = part.astype(bf16)


def total_kernel(parts, out):
    got = parts[...].astype(f32).reshape(8, 8, 8, HD)
    out[...] = jnp.sum(got, axis=1).reshape(64, HD).astype(bf16)


def per_device(queries, pool_keys, pool_values, block_table, ctx_len, out_weight):
    inst = ("z", "x", "c")
    send, where_to = pl.pallas_call(
        route_kernel,
        out_shape=(
            jax.ShapeDtypeStruct((PEERS * MSG, HD), bf16),
            jax.ShapeDtypeStruct((REQS * MAXB,), jnp.int32),
        ),
        in_specs=[HBM, HBM, HBM],
        out_specs=(VMEM, SMEM),
        scratch_shapes=[
            pltpu.SMEM((MAXB, REQS), jnp.int32),
            pltpu.SMEM((REQS,), jnp.int32),
            pltpu.VMEM((REQS, HEADS * HD), bf16),
            pltpu.VMEM((PEERS * MSG, HD), f32),
            pltpu.VMEM((REQS * HEADS, HD), f32),
            pltpu.SMEM((PEERS,), jnp.int32),
            pltpu.SemaphoreType.DMA((3,)),
        ],
        compiler_params=limit,
        name="route",
    )(block_table.T, ctx_len, queries)
    out_weight, send = lax.optimization_barrier((out_weight, send))
    weights = lax.all_gather(out_weight, ("x", "c"), axis=0, tiled=False)
    items = lax.all_to_all(
        send.reshape(PEERS, HEADS + 1, 2, HD), inst, split_axis=0, concat_axis=0, tiled=True
    )
    keys, values = stage(pool_keys, pool_values, name="stage_blocks")
    back = pl.pallas_call(
        attend_kernel,
        out_shape=jax.ShapeDtypeStruct((PEERS * MSG, HD), bf16),
        in_specs=[VMEM, VMEM, VMEM],
        out_specs=VMEM,
        scratch_shapes=[
            pltpu.VMEM((PEERS * MSG, HD), f32),
            pltpu.VMEM((SLOTS * HEADS, HD), f32),
            pltpu.VMEM((SLOTS * HEADS, HD), f32),
        ],
        compiler_params=limit,
        name="attend",
    )(items.reshape(PEERS * MSG, HD), keys, values)
    partials = lax.all_to_all(
        back.reshape(PEERS, HEADS + 1, 2, HD), inst, split_axis=0, concat_axis=0, tiled=True
    )
    attention = pl.pallas_call(
        merge_kernel,
        out_shape=jax.ShapeDtypeStruct((8 * REQS, HEADS * HD), bf16),
        in_specs=[SMEM, VMEM],
        out_specs=VMEM,
        scratch_shapes=[
            pltpu.VMEM((PEERS * MSG, HD), f32),
            pltpu.VMEM((REQS * HEADS, HD), f32),
        ],
        compiler_params=limit,
        name="merge",
    )(where_to, partials.reshape(PEERS * MSG, HD))
    (weights,) = stage(weights, name="stage_weights")
    gathered = lax.all_to_all(
        attention.reshape(8, REQS, HEADS * HD), "z", split_axis=0, concat_axis=0, tiled=True
    )
    parts = pl.pallas_call(
        project_kernel,
        out_shape=jax.ShapeDtypeStruct((512, HD), bf16),
        in_specs=[VMEM, VMEM],
        out_specs=VMEM,
        compiler_params=limit,
        name="project",
    )(gathered.reshape(64, HEADS * HD), weights)
    swapped = lax.all_to_all(
        parts.reshape(64, 8, HD), ("x", "c", "tp"), split_axis=0, concat_axis=0, tiled=True
    )
    return pl.pallas_call(
        total_kernel,
        out_shape=jax.ShapeDtypeStruct((64, HD), bf16),
        in_specs=[VMEM],
        out_specs=VMEM,
        name="total",
    )(swapped.reshape(512, HD))


def solution(mesh):
    split = Mesh(mesh.devices.reshape(8, 4, 2, 8), ("z", "x", "c", "tp"))
    inst = ("z", "x", "c")
    in_specs = (
        P(inst, "tp"),
        P(inst, None, "tp"),
        P(inst, None, "tp"),
        P(inst, None),
        P(inst),
        P("tp", inst),
    )
    return jax.shard_map(
        per_device, mesh=split, in_specs=in_specs, out_specs=P("tp", inst), check_vma=False
    )
```

time: 109 us -> 101 us (0.927)
  blocking collectives: 81.9 us -> 38.9 us
  starting transfers between devices: 0.01 us -> 18.2 us
  waiting for transfers between devices: 0.71 us -> 17.5 us
    all_to_all x3 -> x1, blocking collectives: 61.2 us -> 18.5 us  [per_device(): lax.all_to_all(back.reshape(PEERS, HEADS + 1, 2, HD), inst, split_axis=0,...]
    all_to_all x0 -> x2, starting transfers between devices: none -> 18.2 us  [the longest x1 14.8 us: per_device(): lax.all_to_all(send.reshape(PEERS, HEADS + 1, 2, HD), inst, split_axis=0,...]
    all_to_all x0 -> x2, waiting for transfers between devices: none -> 17.5 us  [the longest x1 11 us: per_device(): lax.all_to_all(send.reshape(PEERS, HEADS + 1, 2, HD), inst, split_axis=0,...]
    unnamed x11 -> x12, local copies, waits for them, and re-layouts: 6.21 us -> 6.08 us
  transfers between devices with their start and end apart: 1 -> 3, of which waited for: 0 -> 2; matrix products, arithmetic and copies ran while one was open for 1% -> 0% of each run, Pallas kernels for 4% -> 3%
where the time goes in v2:
time: 101 us
  blocking collectives  38.9 us (39%)
  starting transfers between devices  18.2 us (18%)
  waiting for transfers between devices  17.5 us (17%)
  between operations  13.5 us (13%)
  Pallas kernels  6.4 us (6%)
  local copies, waits for them, and re-layouts  6.08 us (6%)
    all_to_all x1, blocking collectives, per_device(): lax.all_to_all(parts.reshape(64, 8, HD), ('x', 'c', 'tp'), split_axis=0,...  20.4 us
    all_to_all x1, blocking collectives, per_device(): lax.all_to_all(back.reshape(PEERS, HEADS + 1, 2, HD), inst, split_axis=0,...  18.5 us
    all_to_all x1, starting transfers between devices, per_device(): lax.all_to_all(send.reshape(PEERS, HEADS + 1, 2, HD), inst, split_axis=0,...  14.8 us
    all_to_all x1, waiting for transfers between devices, per_device(): lax.all_to_all(send.reshape(PEERS, HEADS + 1, 2, HD), inst, split_axis=0,...  11 us
    all_to_all x1, waiting for transfers between devices, per_device(): lax.all_to_all(attention.reshape(8, REQS, HEADS * HD), 'z', split_axis=0,...  6.43 us
    unnamed x12, local copies, waits for them, and re-layouts  6.08 us
    all_to_all x1, starting transfers between devices, per_device(): lax.all_to_all(attention.reshape(8, REQS, HEADS * HD), 'z', split_axis=0,...  3.37 us
  transfers between devices with their start and end apart: 3, of which 2 were waited for; matrix products, arithmetic and copies ran while one was open for 0% of the time, Pallas kernels for 3%

profile of v2, /device:TPU:1, one launch (start us, length us, event | category | flops | bytes accessed | tf_op | source)
XLA Modules:
  0.0 100.6 jit_solution(13615862966596846077)
XLA Ops:
  6.5 0.0 all-gather.3.cloned.1.call-start
  6.5 0.0 copy-start.3
  6.5 0.7 copy-done.3
  7.3 0.0 copy-start.4
  7.3 0.7 copy-done.4
  7.9 0.0 copy-start.5
  7.9 0.7 copy-done.5
  8.6 1.5 %route.1 = (bf16[1152,128]{1,0:T(8,128)(2,1)}, s32[32]{0:T(128)S(1)}) custom-call(s32[4,8]{1,0:T(4,128)S(1)} %bitcast.16, s32[8]{0:T(128)S(1)} %copy-done.5, bf16[8,1024]{1,0:T(8,128)(2,1)S(1)} %copy-done.3), custom_call_target="tpu_custom_call" | custom-call | tf_op jit(solution)/shard_map/route/pallas_call | solution.py:202
  10.1 0.0 all-gather.3.cloned.1.call-update
  10.1 14.8 %all-to-all-start = ((bf16[64,9,2,128]{3,2,1,0:T(2,128)(2,1)}), bf16[64,9,2,128]{3,2,1,0:T(2,128)(2,1)S(1)}, u32[]{:S(2)}, u32[]{:S(2)}) async-start(bf16[64,9,2,128]{3,2,1,0:T(2,128)(2,1)} %bitcast.1), calls=%async_computation | async-start | bytes 589824 | tf_op jit(solution)/shard_map/all_to_all | solution.py:224
  25.0 0.0 copy-start.1
  25.0 1.2 %copy-done.1 = bf16[32,128,128]{2,1,0:T(8,128)(2,1)S(1)} copy-done((bf16[32,128,128]{2,1,0:T(8,128)(2,1)S(1)}, bf16[32,128,128]{2,1,0:T(8,128)(2,1)}, u32[]{:S(2)}) %copy-start.1) | copy-done | bytes 1048600
  26.2 0.0 copy-start.2
  26.2 1.2 %copy-done.2 = bf16[32,128,128]{2,1,0:T(8,128)(2,1)S(1)} copy-done((bf16[32,128,128]{2,1,0:T(8,128)(2,1)S(1)}, bf16[32,128,128]{2,1,0:T(8,128)(2,1)}, u32[]{:S(2)}) %copy-start.2) | copy-done | bytes 1048600
  27.5 0.2 stage_blocks.1
  27.7 11.0 %all-to-all-done = bf16[64,9,2,128]{3,2,1,0:T(2,128)(2,1)S(1)} async-done(((bf16[64,9,2,128]{3,2,1,0:T(2,128)(2,1)}), bf16[64,9,2,128]{3,2,1,0:T(2,128)(2,1)S(1)}, u32[]{:S(2)}, u32[]{:S(2)}) %all-to-all-start) | async-done | bytes 294944 | tf_op jit(solution)/shard_map/all_to_all | solution.py:224
  38.7 1.1 %attend.1 = bf16[1152,128]{1,0:T(8,128)(2,1)S(1)} custom-call(bf16[1152,128]{1,0:T(8,128)(2,1)S(1)} %bitcast.12, bf16[32,128,128]{2,1,0:T(8,128)(2,1)S(1)} %get-tuple-element.14.keys, bf16[32,128,128]{2,1,0:T(8,128)(2,1)S(1)} %get-tuple-element.15.values), custom_call_target="tpu_custom_call" | custom-call | tf_op jit(solution)/shard_map/attend/pallas_call | solution.py:228
  39.9 18.5 %all_to_all.20 = bf16[64,9,2,128]{3,2,1,0:T(2,128)(2,1)S(1)} all-to-all(bf16[64,9,2,128]{3,2,1,0:T(2,128)(2,1)S(1)} %bitcast.13), channel_id=1, replica_groups=mesh['z'=8,'x'=4,'c'=2,'tp'=8] {'z','x','c'}, dimensions={0} | all-to-all | bytes 589824 | tf_op jit(solution)/shard_map/all_to_all | solution.py:241
  58.3 1.4 %merge.1 = bf16[64,1024]{1,0:T(8,128)(2,1)} custom-call(s32[32]{0:T(128)S(1)} %get-tuple-element.11.where_to, bf16[1152,128]{1,0:T(8,128)(2,1)S(1)} %bitcast.11), custom_call_target="tpu_custom_call" | custom-call | tf_op jit(solution)/shard_map/merge/pallas_call | solution.py:244
  59.7 3.4 %all-to-all-start.2 = ((bf16[8,8,1024]{2,1,0:T(8,128)(2,1)}), bf16[8,8,1024]{2,1,0:T(8,128)(2,1)S(1)}, u32[]{:S(2)}, u32[]{:S(2)}) async-start(bf16[8,8,1024]{2,1,0:T(8,128)(2,1)} %bitcast.5), calls=%async_computation.2 | async-start | bytes 262144 | tf_op jit(solution)/shard_map/all_to_all | solution.py:257
  63.1 0.0 all-gather.3.cloned.1.call-done
  63.1 0.0 copy-start
  63.1 1.6 %copy-done = bf16[8192,128]{1,0:T(8,128)(2,1)S(1)} copy-done((bf16[8192,128]{1,0:T(8,128)(2,1)S(1)}, bf16[8192,128]{1,0:T(8,128)(2,1)}, u32[]{:S(2)}) %copy-start) | copy-done | bytes 2097176
  64.7 0.2 stage_weights.1.weight
  64.9 6.4 %all-to-all-done.2 = bf16[8,8,1024]{2,1,0:T(8,128)(2,1)S(1)} async-done(((bf16[8,8,1024]{2,1,0:T(8,128)(2,1)}), bf16[8,8,1024]{2,1,0:T(8,128)(2,1)S(1)}, u32[]{:S(2)}, u32[]{:S(2)}) %all-to-all-start.2) | async-done | bytes 131104 | tf_op jit(solution)/shard_map/all_to_all | solution.py:257
  71.3 0.4 project.1
  71.8 20.4 %all_to_all.21 = bf16[64,8,128]{2,1,0:T(8,128)(2,1)} all-to-all(bf16[64,8,128]{2,1,0:T(8,128)(2,1)S(1)} %bitcast.15), channel_id=1, replica_groups=mesh['z'=8,'x'=4,'c'=2,'tp'=8] {'x','c','tp'}, dimensions={0} | all-to-all | bytes 262144 | tf_op jit(solution)/shard_map/all_to_all | solution.py:268
  92.2 1.5 %total.1 = bf16[64,128]{1,0:T(8,128)(2,1)} custom-call(bf16[512,128]{1,0:T(8,128)(2,1)} %bitcast.17), custom_call_target="tpu_custom_call" | custom-call | tf_op jit(solution)/shard_map/total/pallas_call | solution.py:271
Async XLA Ops:
  6.5 56.6 %all-gather.3.cloned.1.call-start = ((), (), s32[]{:S(2)}) async-start(), calls=%async_computation.4 | async-start | bytes 2359296 | tf_op jit(solution)/shard_map/all_gather | solution.py:223
  6.5 0.7 copy-start.3
  7.3 0.7 copy-start.4
  7.9 0.7 copy-start.5
  10.1 28.6 %all-to-all-start = ((bf16[64,9,2,128]{3,2,1,0:T(2,128)(2,1)}), bf16[64,9,2,128]{3,2,1,0:T(2,128)(2,1)S(1)}, u32[]{:S(2)}, u32[]{:S(2)}) async-start(bf16[64,9,2,128]{3,2,1,0:T(2,128)(2,1)} %bitcast.1), calls=%async_computation | async-start | bytes 589824 | tf_op jit(solution)/shard_map/all_to_all | solution.py:224
  25.0 1.2 %copy-start.1 = (bf16[32,128,128]{2,1,0:T(8,128)(2,1)S(1)}, bf16[32,128,128]{2,1,0:T(8,128)(2,1)}, u32[]{:S(2)}) copy-start(bf16[32,128,128]{2,1,0:T(8,128)(2,1)} %refs_0_.1) | copy-start | bytes 3145732
  26.2 1.2 %copy-start.2 = (bf16[32,128,128]{2,1,0:T(8,128)(2,1)S(1)}, bf16[32,128,128]{2,1,0:T(8,128)(2,1)}, u32[]{:S(2)}) copy-start(bf16[32,128,128]{2,1,0:T(8,128)(2,1)} %refs_1_.1) | copy-start | bytes 3145732
  59.7 11.6 %all-to-all-start.2 = ((bf16[8,8,1024]{2,1,0:T(8,128)(2,1)}), bf16[8,8,1024]{2,1,0:T(8,128)(2,1)S(1)}, u32[]{:S(2)}, u32[]{:S(2)}) async-start(bf16[8,8,1024]{2,1,0:T(8,128)(2,1)} %bitcast.5), calls=%async_computation.2 | async-start | bytes 262144 | tf_op jit(solution)/shard_map/all_to_all | solution.py:257
  63.1 1.6 %copy-start = (bf16[8192,128]{1,0:T(8,128)(2,1)S(1)}, bf16[8192,128]{1,0:T(8,128)(2,1)}, u32[]{:S(2)}) copy-start(bf16[8192,128]{1,0:T(8,128)(2,1)} %all-gather.3.cloned.1.call-done) | copy-start | bytes 6291460
Sparse Core Ops, SparseCore 0:
  10.3 37.3 all-gather.2

commit v3 on v2

--- a/solution.py
+++ b/solution.py
@@ -13,59 +13,68 @@
 REQS = 8
 PEERS = 64
 MSG = 18
+ROUTE_LIMIT = 60 * 1024 * 1024
 very_low = -1e30
 f32 = jnp.float32
 bf16 = jnp.bfloat16
 
 VMEM = pl.BlockSpec(memory_space=pltpu.VMEM)
-SMEM = pl.BlockSpec(memory_space=pltpu.SMEM)
 HBM = pl.BlockSpec(memory_space=pltpu.HBM)
 limit = pltpu.CompilerParams(vmem_limit_bytes=24 * 1024 * 1024)
 
 
-def route_kernel(table_in, ctx_in, q_in, out, where_to, table, ctx, q, buf, rows, used, sems):
-    copies = [
-        pltpu.make_async_copy(src, dst, sems.at[n])
-        for n, (src, dst) in enumerate(((table_in, table), (ctx_in, ctx), (q_in, q)))
-    ]
-    for copy in copies:
-        copy.start()
-    buf[...] = jnp.zeros_like(buf)
-    for p in range(PEERS):
-        used[p] = 0
-    for copy in copies:
-        copy.wait()
-    whole = q[...].astype(f32)
-    for h in range(HEADS):
-        rows[pl.ds(h, REQS, stride=HEADS), :] = whole[:, h * HD : (h + 1) * HD]
-    lane = lax.broadcasted_iota(jnp.int32, (1, HD), 1)
-    for e in range(REQS * MAXB):
-        r, b = e // MAXB, e % MAXB
-        slot = table[b, r]
-        p = slot >> 5
-        pos = used[p]
-        used[p] = pos + 1
-        count = jnp.clip(ctx[r] - b * BLOCK, 0, BLOCK)
-        first = p * MSG + pos
-        where_to[e] = first
-        buf[pl.ds(first, HEADS, stride=2), :] = rows[r * 8 : r * 8 + 8, :]
-        note = jnp.where(lane == 0, (slot & 31) + 1, jnp.where(lane == 1, count, 0))
-        buf[pl.ds(first + 16, 1), :] = note.astype(f32)
-    out[...] = buf[...].astype(bf16)
-
-
-def attend_kernel(items, keys, values, out, buf, rows, counts):
-    buf[...] = items[...].astype(f32)
-    notes = jnp.concatenate([buf[pl.ds(16 + i, PEERS, stride=MSG), :] for i in range(2)], axis=0)
-    queries = jnp.concatenate(
+def put_items(buf, items):
+    for i in range(2):
+        for j in range(HEADS + 1):
+            buf[pl.ds(2 * j + i, PEERS, stride=MSG), :] = items[
+                i * PEERS : (i + 1) * PEERS, j * HD : (j + 1) * HD
+            ]
+
+
+def get_items(buf):
+    return jnp.concatenate(
         [
             jnp.concatenate(
-                [buf[pl.ds(2 * h + i, PEERS, stride=MSG), :] for h in range(HEADS)], axis=1
+                [buf[pl.ds(2 * j + i, PEERS, stride=MSG), :] for j in range(HEADS + 1)], axis=1
             )
             for i in range(2)
         ],
         axis=0,
     )
+
+
+def route_kernel(table, ctx, q, out, where_to, buf):
+    entries = REQS * MAXB
+    row = lax.broadcasted_iota(jnp.int32, (entries, HD), 0)
+    lane = lax.broadcasted_iota(jnp.int32, (entries, HD), 1)
+    slot = jnp.concatenate(
+        [jnp.broadcast_to(table[b : b + 1, :], (REQS, REQS)) for b in range(MAXB)], axis=0
+    )
+    length = jnp.broadcast_to(ctx[...], (entries, REQS))
+    own = lane[:, :REQS] == (row[:, :REQS] & 7)
+    slot = jnp.sum(jnp.where(own, slot, 0), axis=1, keepdims=True)
+    length = jnp.sum(jnp.where(own, length, 0), axis=1, keepdims=True)
+    slot = jnp.broadcast_to(slot, (entries, HD))
+    count = jnp.clip(jnp.broadcast_to(length, (entries, HD)) - (row >> 3) * BLOCK, 0, BLOCK)
+    holder = (slot >> 5).astype(f32)
+    holders = jnp.sum(jnp.where(row == lane, holder, 0.0), axis=0, keepdims=True)
+    earlier = jnp.where((holder == holders) & (lane < row), 1.0, 0.0)
+    item = jnp.sum(earlier, axis=1, keepdims=True) * PEERS + holder
+    pick = jnp.where(lane.astype(f32) == item, 1.0, 0.0).astype(bf16)
+    where_to[...] = pick
+    note = jnp.where(lane == 0, (slot & 31) + 1, jnp.where(lane == 1, count, 0)).astype(f32)
+    side = jnp.concatenate([jnp.concatenate([q[...].astype(f32)] * MAXB, axis=0), note], axis=1)
+    items = lax.dot_general(
+        pick, side.astype(bf16), (((0,), (0,)), ((), ())), preferred_element_type=f32
+    )
+    put_items(buf, items)
+    out[...] = buf[...].astype(bf16)
+
+
+def attend_kernel(items, keys, values, out, buf, rows, counts):
+    buf[...] = items[...].astype(f32)
+    given = get_items(buf)
+    queries, notes = given[:, : HEADS * HD], given[:, HEADS * HD :]
     slot_no = lax.broadcasted_iota(jnp.int32, (2 * PEERS, HD), 1).astype(f32) + 1.0
     pick = jnp.where(slot_no == notes[:, :1], 1.0, 0.0).astype(bf16)
     side = jnp.concatenate(
@@ -124,34 +133,27 @@
         [rows[pl.ds(h, SLOTS, stride=HEADS), :] for h in range(HEADS)] + [note], axis=1
     ).astype(bf16)
     back = jnp.dot(pick[:, :SLOTS], side, preferred_element_type=f32)
-    for i in range(2):
-        for j in range(HEADS + 1):
-            buf[pl.ds(2 * j + i, PEERS, stride=MSG), :] = back[
-                i * PEERS : (i + 1) * PEERS, j * HD : (j + 1) * HD
-            ]
+    put_items(buf, back)
     out[...] = buf[...].astype(bf16)
 
 
-def merge_kernel(where_to, items, out, got, rows):
-    got[...] = items[...].astype(f32)
-    lane = lax.broadcasted_iota(jnp.int32, (HEADS, HD), 1)
-    head = lax.broadcasted_iota(jnp.int32, (HEADS, HD), 0)
-    mine = ((lane & 7) == head) & (lane < 24)
-    for r in range(REQS):
-        outs, lses = [], []
-        for b in range(MAXB):
-            first = where_to[r * MAXB + b]
-            outs.append(got[pl.ds(first, HEADS, stride=2), :])
-            note = jnp.broadcast_to(got[pl.ds(first + 16, 1), :], (HEADS, HD))
-            lses.append(jnp.sum(jnp.where(mine, note, 0.0), axis=1, keepdims=True))
-        top = jnp.maximum(jnp.maximum(lses[0], lses[1]), jnp.maximum(lses[2], lses[3]))
-        scales = [jnp.exp(v - top) for v in lses]
-        total = scales[0] + scales[1] + scales[2] + scales[3]
-        merged = sum(s * o for s, o in zip(scales, outs))
-        rows[r * 8 : r * 8 + 8, :] = merged / total
-    whole = jnp.concatenate(
-        [rows[pl.ds(h, REQS, stride=HEADS), :] for h in range(HEADS)], axis=1
-    )
+def merge_kernel(where_to, items, out, buf):
+    buf[...] = items[...].astype(f32)
+    by_entry = jnp.dot(where_to[...], get_items(buf).astype(bf16), preferred_element_type=f32)
+    blocks = [by_entry[b * REQS : (b + 1) * REQS] for b in range(MAXB)]
+    lses = []
+    for block in blocks:
+        note = block[:, HEADS * HD :]
+        lses.append(note[:, :8] + note[:, 8:16] + note[:, 16:24])
+    top = jnp.maximum(jnp.maximum(lses[0], lses[1]), jnp.maximum(lses[2], lses[3]))
+    scales = [jnp.exp(v - top) for v in lses]
+    total = scales[0] + scales[1] + scales[2] + scales[3]
+    scales = [v / total for v in scales]
+    whole = []
+    for h in range(HEADS):
+        at = slice(h * HD, (h + 1) * HD)
+        whole.append(sum(v[:, h : h + 1] * block[:, at] for v, block in zip(scales, blocks)))
+    whole = jnp.concatenate(whole, axis=1)
     out[...] = jnp.concatenate([whole] * 8, axis=0).astype(bf16)
 
 
@@ -203,22 +205,14 @@
         route_kernel,
         out_shape=(
             jax.ShapeDtypeStruct((PEERS * MSG, HD), bf16),
-            jax.ShapeDtypeStruct((REQS * MAXB,), jnp.int32),
+            jax.ShapeDtypeStruct((REQS * MAXB, HD), bf16),
         ),
-        in_specs=[HBM, HBM, HBM],
-        out_specs=(VMEM, SMEM),
-        scratch_shapes=[
-            pltpu.SMEM((MAXB, REQS), jnp.int32),
-            pltpu.SMEM((REQS,), jnp.int32),
-            pltpu.VMEM((REQS, HEADS * HD), bf16),
-            pltpu.VMEM((PEERS * MSG, HD), f32),
-            pltpu.VMEM((REQS * HEADS, HD), f32),
-            pltpu.SMEM((PEERS,), jnp.int32),
-            pltpu.SemaphoreType.DMA((3,)),
-        ],
-        compiler_params=limit,
+        in_specs=[VMEM, VMEM, VMEM],
+        out_specs=(VMEM, VMEM),
+        scratch_shapes=[pltpu.VMEM((PEERS * MSG, HD), f32)],
+        compiler_params=pltpu.CompilerParams(vmem_limit_bytes=ROUTE_LIMIT),
         name="route",
-    )(block_table.T, ctx_len, queries)
+    )(block_table.T, ctx_len[None, :], queries)
     out_weight, send = lax.optimization_barrier((out_weight, send))
     weights = lax.all_gather(out_weight, ("x", "c"), axis=0, tiled=False)
     items = lax.all_to_all(
@@ -244,12 +238,9 @@
     attention = pl.pallas_call(
         merge_kernel,
         out_shape=jax.ShapeDtypeStruct((8 * REQS, HEADS * HD), bf16),
-        in_specs=[SMEM, VMEM],
-        out_specs=VMEM,
-        scratch_shapes=[
-            pltpu.VMEM((PEERS * MSG, HD), f32),
-            pltpu.VMEM((REQS * HEADS, HD), f32),
-        ],
+        in_specs=[VMEM, VMEM],
+        out_specs=VMEM,
+        scratch_shapes=[pltpu.VMEM((PEERS * MSG, HD), f32)],
         compiler_params=limit,
         name="merge",
     )(where_to, partials.reshape(PEERS * MSG, HD))
@@ -273,6 +264,7 @@
         out_shape=jax.ShapeDtypeStruct((64, HD), bf16),
         in_specs=[VMEM],
         out_specs=VMEM,
+        compiler_params=limit,
         name="total",
     )(swapped.reshape(512, HD))
 

time: 101 us -> 98.1 us (0.971)
  local copies, waits for them, and re-layouts: 6.08 us -> 4.03 us
    unnamed x12 -> x8, local copies, waits for them, and re-layouts: 6.08 us -> 4.03 us
where the time goes in v3:
time: 98.1 us; the launch traced here: 97.6 us
  blocking collectives  38.8 us (40%)
  starting transfers between devices  18.2 us (19%)
  waiting for transfers between devices  17.5 us (18%)
  between operations  13.5 us (14%)
  Pallas kernels  5.6 us (6%)
  local copies, waits for them, and re-layouts  4.03 us (4%)
    all_to_all x1, blocking collectives, per_device(): lax.all_to_all(parts.reshape(64, 8, HD), ('x', 'c', 'tp'), split_axis=0,...  20.3 us
    all_to_all x1, blocking collectives, per_device(): lax.all_to_all(back.reshape(PEERS, HEADS + 1, 2, HD), inst, split_axis=0,...  18.5 us
    all_to_all x1, starting transfers between devices, per_device(): lax.all_to_all(send.reshape(PEERS, HEADS + 1, 2, HD), inst, split_axis=0,...  14.8 us
    all_to_all x1, waiting for transfers between devices, per_device(): lax.all_to_all(send.reshape(PEERS, HEADS + 1, 2, HD), inst, split_axis=0,...  11 us
    all_to_all x1, waiting for transfers between devices, per_device(): lax.all_to_all(attention.reshape(8, REQS, HEADS * HD), 'z', split_axis=0,...  6.43 us
    unnamed x8, local copies, waits for them, and re-layouts  4.03 us
    all_to_all x1, starting transfers between devices, per_device(): lax.all_to_all(attention.reshape(8, REQS, HEADS * HD), 'z', split_axis=0,...  3.37 us
  transfers between devices with their start and end apart: 3, of which 2 were waited for; matrix products, arithmetic and copies ran while one was open for 0% of the time, Pallas kernels for 3%

profile of v3, /device:TPU:1, one launch (start us, length us, event | category | flops | bytes accessed | tf_op | source)
XLA Modules:
  0.0 97.6 jit_solution(15491821709593609443)
XLA Ops:
  6.5 0.0 all-gather.3.cloned.1.call-start
  6.5 1.9 %route.1 = (bf16[1152,128]{1,0:T(8,128)(2,1)}, bf16[32,128]{1,0:T(8,128)(2,1)}) custom-call(s32[4,8]{1,0:T(4,128)} %bitcast.19, s32[1,8]{1,0:T(1,128)} %bitcast.20, bf16[8,1024]{1,0:T(8,128)(2,1)} %q.1), custom_call_target="tpu_custom_call" | custom-call | tf_op jit(solution)/shard_map/route/pallas_call | solution.py:204
  8.5 0.0 all-gather.3.cloned.1.call-update
  8.5 14.8 %all-to-all-start = ((bf16[64,9,2,128]{3,2,1,0:T(2,128)(2,1)}), bf16[64,9,2,128]{3,2,1,0:T(2,128)(2,1)S(1)}, u32[]{:S(2)}, u32[]{:S(2)}) async-start(bf16[64,9,2,128]{3,2,1,0:T(2,128)(2,1)} %bitcast.18), calls=%async_computation | async-start | bytes 589824 | tf_op jit(solution)/shard_map/all_to_all | solution.py:218
  23.3 0.0 copy-start.1
  23.4 1.2 %copy-done.1 = bf16[32,128,128]{2,1,0:T(8,128)(2,1)S(1)} copy-done((bf16[32,128,128]{2,1,0:T(8,128)(2,1)S(1)}, bf16[32,128,128]{2,1,0:T(8,128)(2,1)}, u32[]{:S(2)}) %copy-start.1) | copy-done | bytes 1048600
  24.6 0.0 copy-start.2
  24.6 1.2 %copy-done.2 = bf16[32,128,128]{2,1,0:T(8,128)(2,1)S(1)} copy-done((bf16[32,128,128]{2,1,0:T(8,128)(2,1)S(1)}, bf16[32,128,128]{2,1,0:T(8,128)(2,1)}, u32[]{:S(2)}) %copy-start.2) | copy-done | bytes 1048600
  25.8 0.2 stage_blocks.1
  26.0 0.0 copy-start.3
  26.0 11.0 %all-to-all-done = bf16[64,9,2,128]{3,2,1,0:T(2,128)(2,1)S(1)} async-done(((bf16[64,9,2,128]{3,2,1,0:T(2,128)(2,1)}), bf16[64,9,2,128]{3,2,1,0:T(2,128)(2,1)S(1)}, u32[]{:S(2)}, u32[]{:S(2)}) %all-to-all-start) | async-done | bytes 294944 | tf_op jit(solution)/shard_map/all_to_all | solution.py:218
  37.1 1.1 %attend.1 = bf16[1152,128]{1,0:T(8,128)(2,1)S(1)} custom-call(bf16[1152,128]{1,0:T(8,128)(2,1)S(1)} %bitcast.13, bf16[32,128,128]{2,1,0:T(8,128)(2,1)S(1)} %get-tuple-element.14.keys, bf16[32,128,128]{2,1,0:T(8,128)(2,1)S(1)} %get-tuple-element.15.values), custom_call_target="tpu_custom_call" | custom-call | tf_op jit(solution)/shard_map/attend/pallas_call | solution.py:222
  38.2 18.5 %all_to_all.20 = bf16[64,9,2,128]{3,2,1,0:T(2,128)(2,1)S(1)} all-to-all(bf16[64,9,2,128]{3,2,1,0:T(2,128)(2,1)S(1)} %bitcast.14), channel_id=1, replica_groups=mesh['z'=8,'x'=4,'c'=2,'tp'=8] {'z','x','c'}, dimensions={0} | all-to-all | bytes 589824 | tf_op jit(solution)/shard_map/all_to_all | solution.py:235
  56.7 0.0 copy-done.3
  56.7 1.1 %merge.1 = bf16[64,1024]{1,0:T(8,128)(2,1)} custom-call(bf16[32,128]{1,0:T(8,128)(2,1)S(1)} %copy-done.3, bf16[1152,128]{1,0:T(8,128)(2,1)S(1)} %bitcast.12), custom_call_target="tpu_custom_call" | custom-call | tf_op jit(solution)/shard_map/merge/pallas_call | solution.py:238
  57.8 3.4 %all-to-all-start.2 = ((bf16[8,8,1024]{2,1,0:T(8,128)(2,1)}), bf16[8,8,1024]{2,1,0:T(8,128)(2,1)S(1)}, u32[]{:S(2)}, u32[]{:S(2)}) async-start(bf16[8,8,1024]{2,1,0:T(8,128)(2,1)} %bitcast.6), calls=%async_computation.2 | async-start | bytes 262144 | tf_op jit(solution)/shard_map/all_to_all | solution.py:248
  61.1 0.0 all-gather.3.cloned.1.call-done
  61.2 0.0 copy-start
  61.2 1.6 %copy-done = bf16[8192,128]{1,0:T(8,128)(2,1)S(1)} copy-done((bf16[8192,128]{1,0:T(8,128)(2,1)S(1)}, bf16[8192,128]{1,0:T(8,128)(2,1)}, u32[]{:S(2)}) %copy-start) | copy-done | bytes 2097176
  62.8 0.2 stage_weights.1.weight
  62.9 6.4 %all-to-all-done.2 = bf16[8,8,1024]{2,1,0:T(8,128)(2,1)S(1)} async-done(((bf16[8,8,1024]{2,1,0:T(8,128)(2,1)}), bf16[8,8,1024]{2,1,0:T(8,128)(2,1)S(1)}, u32[]{:S(2)}, u32[]{:S(2)}) %all-to-all-start.2) | async-done | bytes 131104 | tf_op jit(solution)/shard_map/all_to_all | solution.py:248
  69.4 0.4 project.1
  69.8 20.3 %all_to_all.21 = bf16[64,8,128]{2,1,0:T(8,128)(2,1)S(1)} all-to-all(bf16[64,8,128]{2,1,0:T(8,128)(2,1)S(1)} %bitcast.16), channel_id=1, replica_groups=mesh['z'=8,'x'=4,'c'=2,'tp'=8] {'x','c','tp'}, dimensions={0} | all-to-all | bytes 262144 | tf_op jit(solution)/shard_map/all_to_all | solution.py:259
  90.1 0.6 total.1
Async XLA Ops:
  6.5 54.6 %all-gather.3.cloned.1.call-start = ((), (), s32[]{:S(2)}) async-start(), calls=%async_computation.4 | async-start | bytes 2359296 | tf_op jit(solution)/shard_map/all_gather | solution.py:217
  8.5 28.6 %all-to-all-start = ((bf16[64,9,2,128]{3,2,1,0:T(2,128)(2,1)}), bf16[64,9,2,128]{3,2,1,0:T(2,128)(2,1)S(1)}, u32[]{:S(2)}, u32[]{:S(2)}) async-start(bf16[64,9,2,128]{3,2,1,0:T(2,128)(2,1)} %bitcast.18), calls=%async_computation | async-start | bytes 589824 | tf_op jit(solution)/shard_map/all_to_all | solution.py:218
  23.3 1.2 %copy-start.1 = (bf16[32,128,128]{2,1,0:T(8,128)(2,1)S(1)}, bf16[32,128,128]{2,1,0:T(8,128)(2,1)}, u32[]{:S(2)}) copy-start(bf16[32,128,128]{2,1,0:T(8,128)(2,1)} %refs_0_.1) | copy-start | bytes 3145732
  24.6 1.2 %copy-start.2 = (bf16[32,128,128]{2,1,0:T(8,128)(2,1)S(1)}, bf16[32,128,128]{2,1,0:T(8,128)(2,1)}, u32[]{:S(2)}) copy-start(bf16[32,128,128]{2,1,0:T(8,128)(2,1)} %refs_1_.1) | copy-start | bytes 3145732
  26.0 30.7 %copy-start.3 = (bf16[32,128]{1,0:T(8,128)(2,1)S(1)}, bf16[32,128]{1,0:T(8,128)(2,1)}, u32[]{:S(2)}) copy-start(bf16[32,128]{1,0:T(8,128)(2,1)} %get-tuple-element.11.where_to) | copy-start | bytes 24580
  57.8 11.6 %all-to-all-start.2 = ((bf16[8,8,1024]{2,1,0:T(8,128)(2,1)}), bf16[8,8,1024]{2,1,0:T(8,128)(2,1)S(1)}, u32[]{:S(2)}, u32[]{:S(2)}) async-start(bf16[8,8,1024]{2,1,0:T(8,128)(2,1)} %bitcast.6), calls=%async_computation.2 | async-start | bytes 262144 | tf_op jit(solution)/shard_map/all_to_all | solution.py:248
  61.2 1.6 %copy-start = (bf16[8192,128]{1,0:T(8,128)(2,1)S(1)}, bf16[8192,128]{1,0:T(8,128)(2,1)}, u32[]{:S(2)}) copy-start(bf16[8192,128]{1,0:T(8,128)(2,1)} %all-gather.3.cloned.1.call-done) | copy-start | bytes 6291460
Sparse Core Ops, SparseCore 0:
  9.5 36.9 all-gather.2

commit v4 on v3

--- a/solution.py
+++ b/solution.py
@@ -154,7 +154,7 @@
         at = slice(h * HD, (h + 1) * HD)
         whole.append(sum(v[:, h : h + 1] * block[:, at] for v, block in zip(scales, blocks)))
     whole = jnp.concatenate(whole, axis=1)
-    out[...] = jnp.concatenate([whole] * 8, axis=0).astype(bf16)
+    out[...] = jnp.concatenate([whole] * 32, axis=0).astype(bf16)
 
 
 def stage_kernel(*refs):
@@ -187,16 +187,17 @@
     )(*arrays)
 
 
-def project_kernel(attention, weight, out):
+def project_kernel(attention, own, other, out):
+    me = lax.axis_index("c")
     left = attention[...]
-    for n in range(8):
-        part = jnp.dot(left, weight[n], preferred_element_type=f32)
-        out[n * 64 : (n + 1) * 64, :] = part.astype(bf16)
+    for c, weight in ((me, own), (1 - me, other)):
+        part = jnp.dot(left, weight[...], preferred_element_type=f32)
+        out[pl.ds(pl.multiple_of(c * 256, 256), 256), :] = part.astype(bf16)
 
 
 def total_kernel(parts, out):
-    got = parts[...].astype(f32).reshape(8, 8, 8, HD)
-    out[...] = jnp.sum(got, axis=1).reshape(64, HD).astype(bf16)
+    got = jnp.sum(parts[...].astype(f32).reshape(2, 8, 4, 8, HD), axis=1)
+    out[...] = jnp.concatenate([got[c, x] for x in range(4) for c in range(2)]).astype(bf16)
 
 
 def per_device(queries, pool_keys, pool_values, block_table, ctx_len, out_weight):
@@ -213,12 +214,13 @@
         compiler_params=pltpu.CompilerParams(vmem_limit_bytes=ROUTE_LIMIT),
         name="route",
     )(block_table.T, ctx_len[None, :], queries)
-    out_weight, send = lax.optimization_barrier((out_weight, send))
-    weights = lax.all_gather(out_weight, ("x", "c"), axis=0, tiled=False)
     items = lax.all_to_all(
         send.reshape(PEERS, HEADS + 1, 2, HD), inst, split_axis=0, concat_axis=0, tiled=True
     )
     keys, values = stage(pool_keys, pool_values, name="stage_blocks")
+    out_weight, keys, values = lax.optimization_barrier((out_weight, keys, values))
+    other_weight = lax.ppermute(out_weight, "c", [(0, 1), (1, 0)])
+    items, other_weight = lax.optimization_barrier((items, other_weight))
     back = pl.pallas_call(
         attend_kernel,
         out_shape=jax.ShapeDtypeStruct((PEERS * MSG, HD), bf16),
@@ -237,27 +239,26 @@
     )
     attention = pl.pallas_call(
         merge_kernel,
-        out_shape=jax.ShapeDtypeStruct((8 * REQS, HEADS * HD), bf16),
+        out_shape=jax.ShapeDtypeStruct((32 * REQS, HEADS * HD), bf16),
         in_specs=[VMEM, VMEM],
         out_specs=VMEM,
         scratch_shapes=[pltpu.VMEM((PEERS * MSG, HD), f32)],
         compiler_params=limit,
         name="merge",
     )(where_to, partials.reshape(PEERS * MSG, HD))
-    (weights,) = stage(weights, name="stage_weights")
     gathered = lax.all_to_all(
-        attention.reshape(8, REQS, HEADS * HD), "z", split_axis=0, concat_axis=0, tiled=True
+        attention.reshape(32, REQS, HEADS * HD), ("z", "x"), split_axis=0, concat_axis=0, tiled=True
     )
     parts = pl.pallas_call(
         project_kernel,
         out_shape=jax.ShapeDtypeStruct((512, HD), bf16),
-        in_specs=[VMEM, VMEM],
+        in_specs=[VMEM] * 3,
         out_specs=VMEM,
         compiler_params=limit,
         name="project",
-    )(gathered.reshape(64, HEADS * HD), weights)
+    )(gathered.reshape(256, HEADS * HD), out_weight, other_weight)
     swapped = lax.all_to_all(
-        parts.reshape(64, 8, HD), ("x", "c", "tp"), split_axis=0, concat_axis=0, tiled=True
+        parts.reshape(16, 32, HD), ("c", "tp"), split_axis=0, concat_axis=0, tiled=True
     )
     return pl.pallas_call(
         total_kernel,

time: 98.1 us -> 88.6 us (0.903)
  blocking collectives: 38.8 us -> 54.9 us
  between operations: 13.5 us -> 0.07 us
  waiting for transfers between devices: 17.5 us -> 7.96 us
  starting transfers between devices: 18.2 us -> 17.2 us
    all_to_all x1 -> x2, blocking collectives: 20.3 us -> 36.5 us  [the longest x1 20 us: per_device(): lax.all_to_all(attention.reshape(32, REQS, HEADS * HD), ('z', 'x'), split...]
    all_to_all x1 -> x0, waiting for transfers between devices: 6.43 us -> none  [per_device(): lax.all_to_all(attention.reshape(8, REQS, HEADS * HD), 'z', split_axis=0,...]
    all_to_all x1, waiting for transfers between devices: 11 us -> 6.82 us  [per_device(): lax.all_to_all(send.reshape(PEERS, HEADS + 1, 2, HD), inst, split_axis=0,...]
    all_to_all x1 -> x0, starting transfers between devices: 3.37 us -> none  [per_device(): lax.all_to_all(attention.reshape(8, REQS, HEADS * HD), 'z', split_axis=0,...]
    ppermute x0 -> x1, starting transfers between devices: none -> 2.35 us  [per_device(): other_weight = lax.ppermute(out_weight, 'c', [(0, 1), (1, 0)])]
    ppermute x0 -> x1, waiting for transfers between devices: none -> 1.14 us  [per_device(): other_weight = lax.ppermute(out_weight, 'c', [(0, 1), (1, 0)])]
  transfers between devices with their start and end apart: 3 -> 2, of which waited for: 2 -> 2; matrix products, arithmetic and copies ran while one was open for 0% -> 0% of each run, Pallas kernels for 3% -> 0%
where the time goes in v4:
time: 88.6 us; the launch traced here: 88.1 us
  blocking collectives  54.9 us (62%)
  starting transfers between devices  17.2 us (19%)
  waiting for transfers between devices  7.96 us (9%)
  Pallas kernels  4.81 us (5%)
  local copies, waits for them, and re-layouts  3.16 us (4%)
    all_to_all x1, blocking collectives, per_device(): lax.all_to_all(attention.reshape(32, REQS, HEADS * HD), ('z', 'x'), split...  20 us
    all_to_all x1, blocking collectives, per_device(): lax.all_to_all(back.reshape(PEERS, HEADS + 1, 2, HD), inst, split_axis=0,...  18.4 us
    all_to_all x1, blocking collectives, per_device(): lax.all_to_all(parts.reshape(16, 32, HD), ('c', 'tp'), split_axis=0, conc...  16.5 us
    all_to_all x1, starting transfers between devices, per_device(): lax.all_to_all(send.reshape(PEERS, HEADS + 1, 2, HD), inst, split_axis=0,...  14.8 us
    all_to_all x1, waiting for transfers between devices, per_device(): lax.all_to_all(send.reshape(PEERS, HEADS + 1, 2, HD), inst, split_axis=0,...  6.82 us
    unnamed x8, local copies, waits for them, and re-layouts  3.16 us
    ppermute x1, starting transfers between devices, per_device(): other_weight = lax.ppermute(out_weight, 'c', [(0, 1), (1, 0)])  2.35 us
    pallas_call x1, Pallas kernels, per_device(): pl.pallas_call(route_kernel, out_shape=(jax.ShapeDtypeStruct((PEERS * MSG...  1.94 us
  transfers between devices with their start and end apart: 2, of which 2 were waited for; matrix products, arithmetic and copies ran while one was open for 0% of the time, Pallas kernels for 0%

profile of v4, /device:TPU:1, one launch (start us, length us, event | category | flops | bytes accessed | tf_op | source)
XLA Modules:
  0.0 88.1 jit_solution(14454972157042926165)
XLA Ops:
  0.0 1.9 %route.1 = (bf16[1152,128]{1,0:T(8,128)(2,1)}, bf16[32,128]{1,0:T(8,128)(2,1)}) custom-call(s32[4,8]{1,0:T(4,128)} %bitcast.18, s32[1,8]{1,0:T(1,128)} %bitcast.19, bf16[8,1024]{1,0:T(8,128)(2,1)} %q.1), custom_call_target="tpu_custom_call" | custom-call | tf_op jit(solution)/shard_map/route/pallas_call | solution.py:205
  1.9 14.8 %all-to-all-start = ((bf16[64,9,2,128]{3,2,1,0:T(2,128)(2,1)}), bf16[64,9,2,128]{3,2,1,0:T(2,128)(2,1)S(1)}, u32[]{:S(2)}, u32[]{:S(2)}) async-start(bf16[64,9,2,128]{3,2,1,0:T(2,128)(2,1)} %bitcast.17), calls=%async_computation | async-start | bytes 589824 | tf_op jit(solution)/shard_map/all_to_all | solution.py:217
  16.8 0.0 copy-start
  16.8 1.2 %copy-done = bf16[32,128,128]{2,1,0:T(8,128)(2,1)S(1)} copy-done((bf16[32,128,128]{2,1,0:T(8,128)(2,1)S(1)}, bf16[32,128,128]{2,1,0:T(8,128)(2,1)}, u32[]{:S(2)}) %copy-start) | copy-done | bytes 1048600
  18.0 0.0 copy-start.1
  18.0 1.2 %copy-done.1 = bf16[32,128,128]{2,1,0:T(8,128)(2,1)S(1)} copy-done((bf16[32,128,128]{2,1,0:T(8,128)(2,1)S(1)}, bf16[32,128,128]{2,1,0:T(8,128)(2,1)}, u32[]{:S(2)}) %copy-start.1) | copy-done | bytes 1048600
  19.2 0.0 copy-start.2
  19.2 0.2 stage_blocks.1
  19.5 0.7 copy-done.2
  20.2 2.4 %collective-permute-start = (bf16[1024,128]{1,0:T(8,128)(2,1)S(1)}, bf16[1024,128]{1,0:T(8,128)(2,1)S(1)}, u32[]{:S(2)}, u32[]{:S(2)}) collective-permute-start(bf16[1024,128]{1,0:T(8,128)(2,1)S(1)} %copy-done.2), channel_id=1, source_target_pairs={{0,8},{8,0},{1,9},{9,1},{2,10},{10,2},{3,11},{11,3},{4,12},{12,4},... | collective-permute-start | bytes 786440 | tf_op jit(solution)/shard_map/ppermute | solution.py:222
  22.5 1.1 %collective-permute-done.other = bf16[1024,128]{1,0:T(8,128)(2,1)S(1)} collective-permute-done((bf16[1024,128]{1,0:T(8,128)(2,1)S(1)}, bf16[1024,128]{1,0:T(8,128)(2,1)S(1)}, u32[]{:S(2)}, u32[]{:S(2)}) %collective-permute-start) | collective-permute-done | bytes 262176 | tf_op jit(solution)/shard_map/ppermute | solution.py:222
  23.7 6.8 %all-to-all-done = bf16[64,9,2,128]{3,2,1,0:T(2,128)(2,1)S(1)} async-done(((bf16[64,9,2,128]{3,2,1,0:T(2,128)(2,1)}), bf16[64,9,2,128]{3,2,1,0:T(2,128)(2,1)S(1)}, u32[]{:S(2)}, u32[]{:S(2)}) %all-to-all-start) | async-done | bytes 294944 | tf_op jit(solution)/shard_map/all_to_all | solution.py:217
  30.5 1.1 %attend.1 = bf16[1152,128]{1,0:T(8,128)(2,1)S(1)} custom-call(bf16[1152,128]{1,0:T(8,128)(2,1)S(1)} %bitcast.13, bf16[32,128,128]{2,1,0:T(8,128)(2,1)S(1)} %get-tuple-element.20.keys, bf16[32,128,128]{2,1,0:T(8,128)(2,1)S(1)} %get-tuple-element.21.values), custom_call_target="tpu_custom_call" | custom-call | tf_op jit(solution)/shard_map/attend/pallas_call | solution.py:224
  31.7 0.0 copy-start.3
  31.7 18.4 %all_to_all.20 = bf16[64,9,2,128]{3,2,1,0:T(2,128)(2,1)S(1)} all-to-all(bf16[64,9,2,128]{3,2,1,0:T(2,128)(2,1)S(1)} %bitcast.14), channel_id=1, replica_groups=mesh['z'=8,'x'=4,'c'=2,'tp'=8] {'z','x','c'}, dimensions={0} | all-to-all | bytes 589824 | tf_op jit(solution)/shard_map/all_to_all | solution.py:237
  50.0 0.0 copy-done.3
  50.0 0.5 merge.1
  50.5 20.0 %all_to_all.21 = bf16[32,8,1024]{2,1,0:T(8,128)(2,1)S(1)} all-to-all(bf16[32,8,1024]{2,1,0:T(8,128)(2,1)S(1)} %bitcast.10), channel_id=1, replica_groups=mesh['z'=8,'x'=4,'c'=2,'tp'=8] {'z','x'}, dimensions={0} | all-to-all | bytes 1048576 | tf_op jit(solution)/shard_map/all_to_all | solution.py:249
  70.5 0.4 project.1
  70.9 16.5 %all_to_all.22 = bf16[16,32,128]{2,1,0:T(8,128)(2,1)S(1)} all-to-all(bf16[16,32,128]{2,1,0:T(8,128)(2,1)S(1)} %bitcast.15), channel_id=1, replica_groups=mesh['z'=8,'x'=4,'c'=2,'tp'=8] {'c','tp'}, dimensions={0} | all-to-all | bytes 262144 | tf_op jit(solution)/shard_map/all_to_all | solution.py:260
  87.5 0.6 total.1
Async XLA Ops:
  1.9 28.6 %all-to-all-start = ((bf16[64,9,2,128]{3,2,1,0:T(2,128)(2,1)}), bf16[64,9,2,128]{3,2,1,0:T(2,128)(2,1)S(1)}, u32[]{:S(2)}, u32[]{:S(2)}) async-start(bf16[64,9,2,128]{3,2,1,0:T(2,128)(2,1)} %bitcast.17), calls=%async_computation | async-start | bytes 589824 | tf_op jit(solution)/shard_map/all_to_all | solution.py:217
  16.8 1.2 %copy-start = (bf16[32,128,128]{2,1,0:T(8,128)(2,1)S(1)}, bf16[32,128,128]{2,1,0:T(8,128)(2,1)}, u32[]{:S(2)}) copy-start(bf16[32,128,128]{2,1,0:T(8,128)(2,1)} %refs_0_.1) | copy-start | bytes 3145732
  18.0 1.2 %copy-start.1 = (bf16[32,128,128]{2,1,0:T(8,128)(2,1)S(1)}, bf16[32,128,128]{2,1,0:T(8,128)(2,1)}, u32[]{:S(2)}) copy-start(bf16[32,128,128]{2,1,0:T(8,128)(2,1)} %refs_1_.1) | copy-start | bytes 3145732
  19.2 0.9 %copy-start.2 = (bf16[1024,128]{1,0:T(8,128)(2,1)S(1)}, bf16[1024,128]{1,0:T(8,128)(2,1)}, u32[]{:S(2)}) copy-start(bf16[1024,128]{1,0:T(8,128)(2,1)} %own) | copy-start | bytes 786436
  20.2 3.5 %collective-permute-start = (bf16[1024,128]{1,0:T(8,128)(2,1)S(1)}, bf16[1024,128]{1,0:T(8,128)(2,1)S(1)}, u32[]{:S(2)}, u32[]{:S(2)}) collective-permute-start(bf16[1024,128]{1,0:T(8,128)(2,1)S(1)} %copy-done.2), channel_id=1, source_target_pairs={{0,8},{8,0},{1,9},{9,1},{2,10},{10,2},{3,11},{11,3},{4,12},{12,4},... | collective-permute-start | bytes 786440 | tf_op jit(solution)/shard_map/ppermute | solution.py:222
  31.7 18.4 %copy-start.3 = (bf16[32,128]{1,0:T(8,128)(2,1)S(1)}, bf16[32,128]{1,0:T(8,128)(2,1)}, u32[]{:S(2)}) copy-start(bf16[32,128]{1,0:T(8,128)(2,1)} %get-tuple-element.14.where_to) | copy-start | bytes 24580

commit v5 on v4

--- a/solution.py
+++ b/solution.py
@@ -56,7 +56,8 @@
     length = jnp.sum(jnp.where(own, length, 0), axis=1, keepdims=True)
     slot = jnp.broadcast_to(slot, (entries, HD))
     count = jnp.clip(jnp.broadcast_to(length, (entries, HD)) - (row >> 3) * BLOCK, 0, BLOCK)
-    holder = (slot >> 5).astype(f32)
+    inst = slot >> 5
+    holder = ((inst & 1) * 32 + (inst >> 3) * 4 + ((inst >> 1) & 3)).astype(f32)
     holders = jnp.sum(jnp.where(row == lane, holder, 0.0), axis=0, keepdims=True)
     earlier = jnp.where((holder == holders) & (lane < row), 1.0, 0.0)
     item = jnp.sum(earlier, axis=1, keepdims=True) * PEERS + holder
@@ -192,6 +193,8 @@
     left = attention[...]
     for c, weight in ((me, own), (1 - me, other)):
         part = jnp.dot(left, weight[...], preferred_element_type=f32)
+        part = part.reshape(4, 8, 8, HD)
+        part = jnp.concatenate([part[x, z] for z in range(8) for x in range(4)])
         out[pl.ds(pl.multiple_of(c * 256, 256), 256), :] = part.astype(bf16)
 
 
@@ -201,7 +204,7 @@
 
 
 def per_device(queries, pool_keys, pool_values, block_table, ctx_len, out_weight):
-    inst = ("z", "x", "c")
+    inst = ("c", "z", "x")
     send, where_to = pl.pallas_call(
         route_kernel,
         out_shape=(
@@ -247,7 +250,7 @@
         name="merge",
     )(where_to, partials.reshape(PEERS * MSG, HD))
     gathered = lax.all_to_all(
-        attention.reshape(32, REQS, HEADS * HD), ("z", "x"), split_axis=0, concat_axis=0, tiled=True
+        attention.reshape(32, REQS, HEADS * HD), ("x", "z"), split_axis=0, concat_axis=0, tiled=True
     )
     parts = pl.pallas_call(
         project_kernel,

time: 88.6 us -> 87.7 us (0.990)
  waiting for transfers between devices: 7.96 us -> 6.92 us
    all_to_all x1, waiting for transfers between devices: 6.82 us -> 5.76 us  [per_device(): lax.all_to_all(send.reshape(PEERS, HEADS + 1, 2, HD), inst, split_axis=0,...]
    all_to_all x1, blocking collectives: 20 us -> 19 us  [per_device(): lax.all_to_all(attention.reshape(32, REQS, HEADS * HD), ('x', 'z'), split...]
    all_to_all x1, blocking collectives: 16.5 us -> 17.5 us  [per_device(): lax.all_to_all(parts.reshape(16, 32, HD), ('c', 'tp'), split_axis=0, conc...]
where the time goes in v5:
time: 87.7 us; the launch traced here: 87 us
  blocking collectives  54.9 us (63%)
  starting transfers between devices  17.2 us (20%)
  waiting for transfers between devices  6.92 us (8%)
  Pallas kernels  4.81 us (5%)
  local copies, waits for them, and re-layouts  3.16 us (4%)
    all_to_all x1, blocking collectives, per_device(): lax.all_to_all(attention.reshape(32, REQS, HEADS * HD), ('x', 'z'), split...  19 us
    all_to_all x1, blocking collectives, per_device(): lax.all_to_all(back.reshape(PEERS, HEADS + 1, 2, HD), inst, split_axis=0,...  18.3 us
    all_to_all x1, blocking collectives, per_device(): lax.all_to_all(parts.reshape(16, 32, HD), ('c', 'tp'), split_axis=0, conc...  17.5 us
    all_to_all x1, starting transfers between devices, per_device(): lax.all_to_all(send.reshape(PEERS, HEADS + 1, 2, HD), inst, split_axis=0,...  14.9 us
    all_to_all x1, waiting for transfers between devices, per_device(): lax.all_to_all(send.reshape(PEERS, HEADS + 1, 2, HD), inst, split_axis=0,...  5.76 us
    unnamed x8, local copies, waits for them, and re-layouts  3.16 us
    ppermute x1, starting transfers between devices, per_device(): other_weight = lax.ppermute(out_weight, 'c', [(0, 1), (1, 0)])  2.25 us
    pallas_call x1, Pallas kernels, per_device(): pl.pallas_call(route_kernel, out_shape=(jax.ShapeDtypeStruct((PEERS * MSG...  1.94 us
  transfers between devices with their start and end apart: 2, of which 2 were waited for; matrix products, arithmetic and copies ran while one was open for 0% of the time, Pallas kernels for 0%

profile of v5, /device:TPU:1, one launch (start us, length us, event | category | flops | bytes accessed | tf_op | source)
XLA Modules:
  0.0 87.0 jit_solution(11758366860666808650)
XLA Ops:
  0.0 1.9 %route.1 = (bf16[1152,128]{1,0:T(8,128)(2,1)}, bf16[32,128]{1,0:T(8,128)(2,1)}) custom-call(s32[4,8]{1,0:T(4,128)} %bitcast.18, s32[1,8]{1,0:T(1,128)} %bitcast.19, bf16[8,1024]{1,0:T(8,128)(2,1)} %q.1), custom_call_target="tpu_custom_call" | custom-call | tf_op jit(solution)/shard_map/route/pallas_call | solution.py:208
  1.9 14.9 %all-to-all-start = ((bf16[64,9,2,128]{3,2,1,0:T(2,128)(2,1)}), bf16[64,9,2,128]{3,2,1,0:T(2,128)(2,1)S(1)}, u32[]{:S(2)}, u32[]{:S(2)}) async-start(bf16[64,9,2,128]{3,2,1,0:T(2,128)(2,1)} %bitcast.17), calls=%async_computation | async-start | bytes 589824 | tf_op jit(solution)/shard_map/all_to_all | solution.py:220
  16.9 0.0 copy-start
  16.9 1.2 %copy-done = bf16[32,128,128]{2,1,0:T(8,128)(2,1)S(1)} copy-done((bf16[32,128,128]{2,1,0:T(8,128)(2,1)S(1)}, bf16[32,128,128]{2,1,0:T(8,128)(2,1)}, u32[]{:S(2)}) %copy-start) | copy-done | bytes 1048600
  18.1 0.0 copy-start.1
  18.1 1.2 %copy-done.1 = bf16[32,128,128]{2,1,0:T(8,128)(2,1)S(1)} copy-done((bf16[32,128,128]{2,1,0:T(8,128)(2,1)S(1)}, bf16[32,128,128]{2,1,0:T(8,128)(2,1)}, u32[]{:S(2)}) %copy-start.1) | copy-done | bytes 1048600
  19.3 0.0 copy-start.2
  19.3 0.2 stage_blocks.1
  19.6 0.7 copy-done.2
  20.3 2.3 %collective-permute-start = (bf16[1024,128]{1,0:T(8,128)(2,1)S(1)}, bf16[1024,128]{1,0:T(8,128)(2,1)S(1)}, u32[]{:S(2)}, u32[]{:S(2)}) collective-permute-start(bf16[1024,128]{1,0:T(8,128)(2,1)S(1)} %copy-done.2), channel_id=1, source_target_pairs={{0,8},{8,0},{1,9},{9,1},{2,10},{10,2},{3,11},{11,3},{4,12},{12,4},... | collective-permute-start | bytes 786440 | tf_op jit(solution)/shard_map/ppermute | solution.py:225
  22.5 1.2 %collective-permute-done.other = bf16[1024,128]{1,0:T(8,128)(2,1)S(1)} collective-permute-done((bf16[1024,128]{1,0:T(8,128)(2,1)S(1)}, bf16[1024,128]{1,0:T(8,128)(2,1)S(1)}, u32[]{:S(2)}, u32[]{:S(2)}) %collective-permute-start) | collective-permute-done | bytes 262176 | tf_op jit(solution)/shard_map/ppermute | solution.py:225
  23.7 5.8 %all-to-all-done = bf16[64,9,2,128]{3,2,1,0:T(2,128)(2,1)S(1)} async-done(((bf16[64,9,2,128]{3,2,1,0:T(2,128)(2,1)}), bf16[64,9,2,128]{3,2,1,0:T(2,128)(2,1)S(1)}, u32[]{:S(2)}, u32[]{:S(2)}) %all-to-all-start) | async-done | bytes 294944 | tf_op jit(solution)/shard_map/all_to_all | solution.py:220
  29.5 1.1 %attend.1 = bf16[1152,128]{1,0:T(8,128)(2,1)S(1)} custom-call(bf16[1152,128]{1,0:T(8,128)(2,1)S(1)} %bitcast.13, bf16[32,128,128]{2,1,0:T(8,128)(2,1)S(1)} %get-tuple-element.20.keys, bf16[32,128,128]{2,1,0:T(8,128)(2,1)S(1)} %get-tuple-element.21.values), custom_call_target="tpu_custom_call" | custom-call | tf_op jit(solution)/shard_map/attend/pallas_call | solution.py:227
  30.6 0.0 copy-start.3
  30.6 18.3 %all_to_all.20 = bf16[64,9,2,128]{3,2,1,0:T(2,128)(2,1)S(1)} all-to-all(bf16[64,9,2,128]{3,2,1,0:T(2,128)(2,1)S(1)} %bitcast.14), channel_id=1, replica_groups=mesh['z'=8,'x'=4,'c'=2,'tp'=8] {'c','z','x'}, dimensions={0} | all-to-all | bytes 589824 | tf_op jit(solution)/shard_map/all_to_all | solution.py:240
  49.0 0.0 copy-done.3
  49.0 0.5 merge.1
  49.4 19.0 %all_to_all.21 = bf16[32,8,1024]{2,1,0:T(8,128)(2,1)S(1)} all-to-all(bf16[32,8,1024]{2,1,0:T(8,128)(2,1)S(1)} %bitcast.10), channel_id=1, replica_groups=mesh['z'=8,'x'=4,'c'=2,'tp'=8] {'x','z'}, dimensions={0} | all-to-all | bytes 1048576 | tf_op jit(solution)/shard_map/all_to_all | solution.py:252
  68.5 0.4 project.1
  68.9 17.5 %all_to_all.22 = bf16[16,32,128]{2,1,0:T(8,128)(2,1)S(1)} all-to-all(bf16[16,32,128]{2,1,0:T(8,128)(2,1)S(1)} %bitcast.15), channel_id=1, replica_groups=mesh['z'=8,'x'=4,'c'=2,'tp'=8] {'c','tp'}, dimensions={0} | all-to-all | bytes 262144 | tf_op jit(solution)/shard_map/all_to_all | solution.py:263
  86.4 0.6 total.1
Async XLA Ops:
  1.9 27.5 %all-to-all-start = ((bf16[64,9,2,128]{3,2,1,0:T(2,128)(2,1)}), bf16[64,9,2,128]{3,2,1,0:T(2,128)(2,1)S(1)}, u32[]{:S(2)}, u32[]{:S(2)}) async-start(bf16[64,9,2,128]{3,2,1,0:T(2,128)(2,1)} %bitcast.17), calls=%async_computation | async-start | bytes 589824 | tf_op jit(solution)/shard_map/all_to_all | solution.py:220
  16.9 1.2 %copy-start = (bf16[32,128,128]{2,1,0:T(8,128)(2,1)S(1)}, bf16[32,128,128]{2,1,0:T(8,128)(2,1)}, u32[]{:S(2)}) copy-start(bf16[32,128,128]{2,1,0:T(8,128)(2,1)} %refs_0_.1) | copy-start | bytes 3145732
  18.1 1.2 %copy-start.1 = (bf16[32,128,128]{2,1,0:T(8,128)(2,1)S(1)}, bf16[32,128,128]{2,1,0:T(8,128)(2,1)}, u32[]{:S(2)}) copy-start(bf16[32,128,128]{2,1,0:T(8,128)(2,1)} %refs_1_.1) | copy-start | bytes 3145732
  19.3 0.9 %copy-start.2 = (bf16[1024,128]{1,0:T(8,128)(2,1)S(1)}, bf16[1024,128]{1,0:T(8,128)(2,1)}, u32[]{:S(2)}) copy-start(bf16[1024,128]{1,0:T(8,128)(2,1)} %own) | copy-start | bytes 786436
  20.3 3.4 %collective-permute-start = (bf16[1024,128]{1,0:T(8,128)(2,1)S(1)}, bf16[1024,128]{1,0:T(8,128)(2,1)S(1)}, u32[]{:S(2)}, u32[]{:S(2)}) collective-permute-start(bf16[1024,128]{1,0:T(8,128)(2,1)S(1)} %copy-done.2), channel_id=1, source_target_pairs={{0,8},{8,0},{1,9},{9,1},{2,10},{10,2},{3,11},{11,3},{4,12},{12,4},... | collective-permute-start | bytes 786440 | tf_op jit(solution)/shard_map/ppermute | solution.py:225
  30.6 18.4 %copy-start.3 = (bf16[32,128]{1,0:T(8,128)(2,1)S(1)}, bf16[32,128]{1,0:T(8,128)(2,1)}, u32[]{:S(2)}) copy-start(bf16[32,128]{1,0:T(8,128)(2,1)} %get-tuple-element.14.where_to) | copy-start | bytes 24580

commit v6 on v5

--- a/solution.py
+++ b/solution.py
@@ -13,6 +13,7 @@
 REQS = 8
 PEERS = 64
 MSG = 18
+ROWS = PEERS * MSG
 ROUTE_LIMIT = 60 * 1024 * 1024
 very_low = -1e30
 f32 = jnp.float32
@@ -69,11 +70,11 @@
         pick, side.astype(bf16), (((0,), (0,)), ((), ())), preferred_element_type=f32
     )
     put_items(buf, items)
-    out[...] = buf[...].astype(bf16)
+    out[...] = buf[:ROWS, :].astype(bf16)
 
 
 def attend_kernel(items, keys, values, out, buf, rows, counts):
-    buf[...] = items[...].astype(f32)
+    buf[:ROWS, :] = items[...].astype(f32)
     given = get_items(buf)
     queries, notes = given[:, : HEADS * HD], given[:, HEADS * HD :]
     slot_no = lax.broadcasted_iota(jnp.int32, (2 * PEERS, HD), 1).astype(f32) + 1.0
@@ -82,8 +83,8 @@
         [queries, jnp.broadcast_to(notes[:, 1:2], (2 * PEERS, HD))], axis=1
     ).astype(bf16)
     by_slot = lax.dot_general(
-        pick, side, (((0,), (0,)), ((), ())), preferred_element_type=f32
-    )[:SLOTS]
+        pick[:, :SLOTS], side, (((0,), (0,)), ((), ())), preferred_element_type=f32
+    )
     for h in range(HEADS):
         rows[pl.ds(h, SLOTS, stride=HEADS), :] = by_slot[:, h * HD : (h + 1) * HD]
         counts[pl.ds(h, SLOTS, stride=HEADS), :] = by_slot[:, HEADS * HD :]
@@ -98,7 +99,7 @@
         parts += [pair[:8, :BLOCK], pair[8:, BLOCK:]]
     scores = jnp.concatenate(parts, axis=0) * HD ** (-0.5)
     token = lax.broadcasted_iota(jnp.int32, scores.shape, 1).astype(f32)
-    usable = token < counts[...]
+    usable = token < counts[: SLOTS * HEADS, :]
     scores = jnp.where(usable, scores, very_low)
     top = jnp.max(scores, axis=1, keepdims=True)
     weights = jnp.where(usable, jnp.exp(scores - top), 0.0)
@@ -117,7 +118,7 @@
         )
     alive = total > 0.0
     safe = jnp.where(alive, total, 1.0)
-    rows[...] = jnp.concatenate(parts, axis=0) / safe
+    rows[: SLOTS * HEADS, :] = jnp.concatenate(parts, axis=0) / safe
     lse = jnp.where(alive, top + jnp.log(safe), very_low)
     high = lse.astype(bf16).astype(f32)
     mid = (lse - high).astype(bf16).astype(f32)
@@ -135,11 +136,11 @@
     ).astype(bf16)
     back = jnp.dot(pick[:, :SLOTS], side, preferred_element_type=f32)
     put_items(buf, back)
-    out[...] = buf[...].astype(bf16)
+    out[...] = buf[:ROWS, :].astype(bf16)
 
 
 def merge_kernel(where_to, items, out, buf):
-    buf[...] = items[...].astype(f32)
+    buf[:ROWS, :] = items[...].astype(f32)
     by_entry = jnp.dot(where_to[...], get_items(buf).astype(bf16), preferred_element_type=f32)
     blocks = [by_entry[b * REQS : (b + 1) * REQS] for b in range(MAXB)]
     lses = []
@@ -208,12 +209,12 @@
     send, where_to = pl.pallas_call(
         route_kernel,
         out_shape=(
-            jax.ShapeDtypeStruct((PEERS * MSG, HD), bf16),
+            jax.ShapeDtypeStruct((ROWS, HD), bf16),
             jax.ShapeDtypeStruct((REQS * MAXB, HD), bf16),
         ),
         in_specs=[VMEM, VMEM, VMEM],
         out_specs=(VMEM, VMEM),
-        scratch_shapes=[pltpu.VMEM((PEERS * MSG, HD), f32)],
+        scratch_shapes=[pltpu.VMEM((ROWS + 32, HD), f32)],
         compiler_params=pltpu.CompilerParams(vmem_limit_bytes=ROUTE_LIMIT),
         name="route",
     )(block_table.T, ctx_len[None, :], queries)
@@ -226,17 +227,17 @@
     items, other_weight = lax.optimization_barrier((items, other_weight))
     back = pl.pallas_call(
         attend_kernel,
-        out_shape=jax.ShapeDtypeStruct((PEERS * MSG, HD), bf16),
+        out_shape=jax.ShapeDtypeStruct((ROWS, HD), bf16),
         in_specs=[VMEM, VMEM, VMEM],
         out_specs=VMEM,
         scratch_shapes=[
-            pltpu.VMEM((PEERS * MSG, HD), f32),
-            pltpu.VMEM((SLOTS * HEADS, HD), f32),
-            pltpu.VMEM((SLOTS * HEADS, HD), f32),
+            pltpu.VMEM((ROWS + 32, HD), f32),
+            pltpu.VMEM((SLOTS * HEADS + 16, HD), f32),
+            pltpu.VMEM((SLOTS * HEADS + 16, HD), f32),
         ],
         compiler_params=limit,
         name="attend",
-    )(items.reshape(PEERS * MSG, HD), keys, values)
+    )(items.reshape(ROWS, HD), keys, values)
     partials = lax.all_to_all(
         back.reshape(PEERS, HEADS + 1, 2, HD), inst, split_axis=0, concat_axis=0, tiled=True
     )
@@ -245,10 +246,10 @@
         out_shape=jax.ShapeDtypeStruct((32 * REQS, HEADS * HD), bf16),
         in_specs=[VMEM, VMEM],
         out_specs=VMEM,
-        scratch_shapes=[pltpu.VMEM((PEERS * MSG, HD), f32)],
+        scratch_shapes=[pltpu.VMEM((ROWS + 32, HD), f32)],
         compiler_params=limit,
         name="merge",
-    )(where_to, partials.reshape(PEERS * MSG, HD))
+    )(where_to, partials.reshape(ROWS, HD))
     gathered = lax.all_to_all(
         attention.reshape(32, REQS, HEADS * HD), ("x", "z"), split_axis=0, concat_axis=0, tiled=True
     )

time: 87.7 us -> 87.7 us (level)
  no operation moved by 1% of the time
where the time goes in v6:
time: 87.7 us; the launch traced here: 87 us
  blocking collectives  54.9 us (63%)
  starting transfers between devices  17.2 us (20%)
  waiting for transfers between devices  6.92 us (8%)
  Pallas kernels  4.8 us (5%)
  local copies, waits for them, and re-layouts  3.16 us (4%)
    all_to_all x1, blocking collectives, per_device(): lax.all_to_all(attention.reshape(32, REQS, HEADS * HD), ('x', 'z'), split...  19 us
    all_to_all x1, blocking collectives, per_device(): lax.all_to_all(back.reshape(PEERS, HEADS + 1, 2, HD), inst, split_axis=0,...  18.4 us
    all_to_all x1, blocking collectives, per_device(): lax.all_to_all(parts.reshape(16, 32, HD), ('c', 'tp'), split_axis=0, conc...  17.5 us
    all_to_all x1, starting transfers between devices, per_device(): lax.all_to_all(send.reshape(PEERS, HEADS + 1, 2, HD), inst, split_axis=0,...  14.9 us
    all_to_all x1, waiting for transfers between devices, per_device(): lax.all_to_all(send.reshape(PEERS, HEADS + 1, 2, HD), inst, split_axis=0,...  5.76 us
    unnamed x8, local copies, waits for them, and re-layouts  3.16 us
    ppermute x1, starting transfers between devices, per_device(): other_weight = lax.ppermute(out_weight, 'c', [(0, 1), (1, 0)])  2.25 us
    pallas_call x1, Pallas kernels, per_device(): pl.pallas_call(route_kernel, out_shape=(jax.ShapeDtypeStruct((ROWS, HD),...  1.94 us
  transfers between devices with their start and end apart: 2, of which 2 were waited for; matrix products, arithmetic and copies ran while one was open for 0% of the time, Pallas kernels for 0%

profile of v6, /device:TPU:1, one launch (start us, length us, event | category | flops | bytes accessed | tf_op | source)
XLA Modules:
  0.0 87.0 jit_solution(14277382773980871426)
XLA Ops:
  0.0 1.9 %route.1 = (bf16[1152,128]{1,0:T(8,128)(2,1)}, bf16[32,128]{1,0:T(8,128)(2,1)}) custom-call(s32[4,8]{1,0:T(4,128)} %bitcast.18, s32[1,8]{1,0:T(1,128)} %bitcast.19, bf16[8,1024]{1,0:T(8,128)(2,1)} %q.1), custom_call_target="tpu_custom_call" | custom-call | tf_op jit(solution)/shard_map/route/pallas_call | solution.py:209
  1.9 14.9 %all-to-all-start = ((bf16[64,9,2,128]{3,2,1,0:T(2,128)(2,1)}), bf16[64,9,2,128]{3,2,1,0:T(2,128)(2,1)S(1)}, u32[]{:S(2)}, u32[]{:S(2)}) async-start(bf16[64,9,2,128]{3,2,1,0:T(2,128)(2,1)} %bitcast.17), calls=%async_computation | async-start | bytes 589824 | tf_op jit(solution)/shard_map/all_to_all | solution.py:221
  16.9 0.0 copy-start
  16.9 1.2 %copy-done = bf16[32,128,128]{2,1,0:T(8,128)(2,1)S(1)} copy-done((bf16[32,128,128]{2,1,0:T(8,128)(2,1)S(1)}, bf16[32,128,128]{2,1,0:T(8,128)(2,1)}, u32[]{:S(2)}) %copy-start) | copy-done | bytes 1048600
  18.1 0.0 copy-start.1
  18.1 1.2 %copy-done.1 = bf16[32,128,128]{2,1,0:T(8,128)(2,1)S(1)} copy-done((bf16[32,128,128]{2,1,0:T(8,128)(2,1)S(1)}, bf16[32,128,128]{2,1,0:T(8,128)(2,1)}, u32[]{:S(2)}) %copy-start.1) | copy-done | bytes 1048600
  19.3 0.0 copy-start.2
  19.3 0.2 stage_blocks.1
  19.6 0.7 copy-done.2
  20.3 2.3 %collective-permute-start = (bf16[1024,128]{1,0:T(8,128)(2,1)S(1)}, bf16[1024,128]{1,0:T(8,128)(2,1)S(1)}, u32[]{:S(2)}, u32[]{:S(2)}) collective-permute-start(bf16[1024,128]{1,0:T(8,128)(2,1)S(1)} %copy-done.2), channel_id=1, source_target_pairs={{0,8},{8,0},{1,9},{9,1},{2,10},{10,2},{3,11},{11,3},{4,12},{12,4},... | collective-permute-start | bytes 786440 | tf_op jit(solution)/shard_map/ppermute | solution.py:226
  22.5 1.2 %collective-permute-done.other = bf16[1024,128]{1,0:T(8,128)(2,1)S(1)} collective-permute-done((bf16[1024,128]{1,0:T(8,128)(2,1)S(1)}, bf16[1024,128]{1,0:T(8,128)(2,1)S(1)}, u32[]{:S(2)}, u32[]{:S(2)}) %collective-permute-start) | collective-permute-done | bytes 262176 | tf_op jit(solution)/shard_map/ppermute | solution.py:226
  23.7 5.8 %all-to-all-done = bf16[64,9,2,128]{3,2,1,0:T(2,128)(2,1)S(1)} async-done(((bf16[64,9,2,128]{3,2,1,0:T(2,128)(2,1)}), bf16[64,9,2,128]{3,2,1,0:T(2,128)(2,1)S(1)}, u32[]{:S(2)}, u32[]{:S(2)}) %all-to-all-start) | async-done | bytes 294944 | tf_op jit(solution)/shard_map/all_to_all | solution.py:221
  29.5 1.1 %attend.1 = bf16[1152,128]{1,0:T(8,128)(2,1)S(1)} custom-call(bf16[1152,128]{1,0:T(8,128)(2,1)S(1)} %bitcast.13, bf16[32,128,128]{2,1,0:T(8,128)(2,1)S(1)} %get-tuple-element.20.keys, bf16[32,128,128]{2,1,0:T(8,128)(2,1)S(1)} %get-tuple-element.21.values), custom_call_target="tpu_custom_call" | custom-call | tf_op jit(solution)/shard_map/attend/pallas_call | solution.py:228
  30.6 0.0 copy-start.3
  30.6 18.4 %all_to_all.20 = bf16[64,9,2,128]{3,2,1,0:T(2,128)(2,1)S(1)} all-to-all(bf16[64,9,2,128]{3,2,1,0:T(2,128)(2,1)S(1)} %bitcast.14), channel_id=1, replica_groups=mesh['z'=8,'x'=4,'c'=2,'tp'=8] {'c','z','x'}, dimensions={0} | all-to-all | bytes 589824 | tf_op jit(solution)/shard_map/all_to_all | solution.py:241
  49.0 0.0 copy-done.3
  49.0 0.5 merge.1
  49.4 19.0 %all_to_all.21 = bf16[32,8,1024]{2,1,0:T(8,128)(2,1)S(1)} all-to-all(bf16[32,8,1024]{2,1,0:T(8,128)(2,1)S(1)} %bitcast.10), channel_id=1, replica_groups=mesh['z'=8,'x'=4,'c'=2,'tp'=8] {'x','z'}, dimensions={0} | all-to-all | bytes 1048576 | tf_op jit(solution)/shard_map/all_to_all | solution.py:253
  68.5 0.4 project.1
  68.9 17.5 %all_to_all.22 = bf16[16,32,128]{2,1,0:T(8,128)(2,1)S(1)} all-to-all(bf16[16,32,128]{2,1,0:T(8,128)(2,1)S(1)} %bitcast.15), channel_id=1, replica_groups=mesh['z'=8,'x'=4,'c'=2,'tp'=8] {'c','tp'}, dimensions={0} | all-to-all | bytes 262144 | tf_op jit(solution)/shard_map/all_to_all | solution.py:264
  86.4 0.6 total.1
Async XLA Ops:
  1.9 27.5 %all-to-all-start = ((bf16[64,9,2,128]{3,2,1,0:T(2,128)(2,1)}), bf16[64,9,2,128]{3,2,1,0:T(2,128)(2,1)S(1)}, u32[]{:S(2)}, u32[]{:S(2)}) async-start(bf16[64,9,2,128]{3,2,1,0:T(2,128)(2,1)} %bitcast.17), calls=%async_computation | async-start | bytes 589824 | tf_op jit(solution)/shard_map/all_to_all | solution.py:221
  16.9 1.2 %copy-start = (bf16[32,128,128]{2,1,0:T(8,128)(2,1)S(1)}, bf16[32,128,128]{2,1,0:T(8,128)(2,1)}, u32[]{:S(2)}) copy-start(bf16[32,128,128]{2,1,0:T(8,128)(2,1)} %refs_0_.1) | copy-start | bytes 3145732
  18.1 1.2 %copy-start.1 = (bf16[32,128,128]{2,1,0:T(8,128)(2,1)S(1)}, bf16[32,128,128]{2,1,0:T(8,128)(2,1)}, u32[]{:S(2)}) copy-start(bf16[32,128,128]{2,1,0:T(8,128)(2,1)} %refs_1_.1) | copy-start | bytes 3145732
  19.3 0.9 %copy-start.2 = (bf16[1024,128]{1,0:T(8,128)(2,1)S(1)}, bf16[1024,128]{1,0:T(8,128)(2,1)}, u32[]{:S(2)}) copy-start(bf16[1024,128]{1,0:T(8,128)(2,1)} %own) | copy-start | bytes 786436
  20.3 3.4 %collective-permute-start = (bf16[1024,128]{1,0:T(8,128)(2,1)S(1)}, bf16[1024,128]{1,0:T(8,128)(2,1)S(1)}, u32[]{:S(2)}, u32[]{:S(2)}) collective-permute-start(bf16[1024,128]{1,0:T(8,128)(2,1)S(1)} %copy-done.2), channel_id=1, source_target_pairs={{0,8},{8,0},{1,9},{9,1},{2,10},{10,2},{3,11},{11,3},{4,12},{12,4},... | collective-permute-start | bytes 786440 | tf_op jit(solution)/shard_map/ppermute | solution.py:226
  30.6 18.4 %copy-start.3 = (bf16[32,128]{1,0:T(8,128)(2,1)S(1)}, bf16[32,128]{1,0:T(8,128)(2,1)}, u32[]{:S(2)}) copy-start(bf16[32,128]{1,0:T(8,128)(2,1)} %get-tuple-element.14.where_to) | copy-start | bytes 24580

commit v7 on v6

--- a/solution.py
+++ b/solution.py
@@ -8,11 +8,12 @@
 HD = 128
 BLOCK = 128
 MAXB = 4
-SLOTS = 32
+SLOTS = 64
 HEADS = 8
 REQS = 8
-PEERS = 64
-MSG = 18
+PEERS = 32
+PER = 4
+MSG = 9 * PER
 ROWS = PEERS * MSG
 ROUTE_LIMIT = 60 * 1024 * 1024
 very_low = -1e30
@@ -21,13 +22,13 @@
 
 VMEM = pl.BlockSpec(memory_space=pltpu.VMEM)
 HBM = pl.BlockSpec(memory_space=pltpu.HBM)
-limit = pltpu.CompilerParams(vmem_limit_bytes=24 * 1024 * 1024)
+limit = pltpu.CompilerParams(vmem_limit_bytes=16 * 1024 * 1024)
 
 
 def put_items(buf, items):
-    for i in range(2):
+    for i in range(PER):
         for j in range(HEADS + 1):
-            buf[pl.ds(2 * j + i, PEERS, stride=MSG), :] = items[
+            buf[pl.ds(PER * j + i, PEERS, stride=MSG), :] = items[
                 i * PEERS : (i + 1) * PEERS, j * HD : (j + 1) * HD
             ]
 
@@ -36,9 +37,9 @@
     return jnp.concatenate(
         [
             jnp.concatenate(
-                [buf[pl.ds(2 * j + i, PEERS, stride=MSG), :] for j in range(HEADS + 1)], axis=1
+                [buf[pl.ds(PER * j + i, PEERS, stride=MSG), :] for j in range(HEADS + 1)], axis=1
             )
-            for i in range(2)
+            for i in range(PER)
         ],
         axis=0,
     )
@@ -58,13 +59,15 @@
     slot = jnp.broadcast_to(slot, (entries, HD))
     count = jnp.clip(jnp.broadcast_to(length, (entries, HD)) - (row >> 3) * BLOCK, 0, BLOCK)
     inst = slot >> 5
-    holder = ((inst & 1) * 32 + (inst >> 3) * 4 + ((inst >> 1) & 3)).astype(f32)
+    holder = inst.astype(f32)
     holders = jnp.sum(jnp.where(row == lane, holder, 0.0), axis=0, keepdims=True)
     earlier = jnp.where((holder == holders) & (lane < row), 1.0, 0.0)
-    item = jnp.sum(earlier, axis=1, keepdims=True) * PEERS + holder
+    away = (inst & 1) ^ lax.axis_index("c")
+    place = (away * 2 * PEERS + (inst >> 1)).astype(f32)
+    item = jnp.sum(earlier, axis=1, keepdims=True) * PEERS + place
     pick = jnp.where(lane.astype(f32) == item, 1.0, 0.0).astype(bf16)
     where_to[...] = pick
-    note = jnp.where(lane == 0, (slot & 31) + 1, jnp.where(lane == 1, count, 0)).astype(f32)
+    note = jnp.where(lane == 0, away * 32 + (slot & 31) + 1, jnp.where(lane == 1, count, 0)).astype(f32)
     side = jnp.concatenate([jnp.concatenate([q[...].astype(f32)] * MAXB, axis=0), note], axis=1)
     items = lax.dot_general(
         pick, side.astype(bf16), (((0,), (0,)), ((), ())), preferred_element_type=f32
@@ -73,18 +76,23 @@
     out[...] = buf[:ROWS, :].astype(bf16)
 
 
-def attend_kernel(items, keys, values, out, buf, rows, counts):
+def unpack_kernel(items, picks, slots, buf):
     buf[:ROWS, :] = items[...].astype(f32)
     given = get_items(buf)
     queries, notes = given[:, : HEADS * HD], given[:, HEADS * HD :]
-    slot_no = lax.broadcasted_iota(jnp.int32, (2 * PEERS, HD), 1).astype(f32) + 1.0
+    slot_no = lax.broadcasted_iota(jnp.int32, (PER * PEERS, HD), 1).astype(f32) + 1.0
     pick = jnp.where(slot_no == notes[:, :1], 1.0, 0.0).astype(bf16)
     side = jnp.concatenate(
-        [queries, jnp.broadcast_to(notes[:, 1:2], (2 * PEERS, HD))], axis=1
+        [queries, jnp.broadcast_to(notes[:, 1:2], (PER * PEERS, HD))], axis=1
     ).astype(bf16)
     by_slot = lax.dot_general(
         pick[:, :SLOTS], side, (((0,), (0,)), ((), ())), preferred_element_type=f32
     )
+    picks[...] = pick
+    slots[...] = by_slot
+
+
+def attend_kernel(pick, by_slot, keys, values, other_keys, other_values, out, buf, rows, counts):
     for h in range(HEADS):
         rows[pl.ds(h, SLOTS, stride=HEADS), :] = by_slot[:, h * HD : (h + 1) * HD]
         counts[pl.ds(h, SLOTS, stride=HEADS), :] = by_slot[:, HEADS * HD :]
@@ -92,7 +100,7 @@
     for s in range(0, SLOTS, 2):
         pair = lax.dot_general(
             rows[s * 8 : s * 8 + 16, :].astype(bf16),
-            keys[s : s + 2].reshape(2 * BLOCK, HD),
+            (keys if s < 32 else other_keys)[s % 32 : s % 32 + 2].reshape(2 * BLOCK, HD),
             (((1,), (1,)), ((), ())),
             preferred_element_type=f32,
         )
@@ -112,7 +120,7 @@
         parts.append(
             jnp.dot(
                 jnp.concatenate([first, second], axis=0).astype(bf16),
-                values[s : s + 2].reshape(2 * BLOCK, HD),
+                (values if s < 32 else other_values)[s % 32 : s % 32 + 2].reshape(2 * BLOCK, HD),
                 preferred_element_type=f32,
             )
         )
@@ -205,7 +213,7 @@
 
 
 def per_device(queries, pool_keys, pool_values, block_table, ctx_len, out_weight):
-    inst = ("c", "z", "x")
+    inst = ("z", "x")
     send, where_to = pl.pallas_call(
         route_kernel,
         out_shape=(
@@ -214,39 +222,57 @@
         ),
         in_specs=[VMEM, VMEM, VMEM],
         out_specs=(VMEM, VMEM),
-        scratch_shapes=[pltpu.VMEM((ROWS + 32, HD), f32)],
+        scratch_shapes=[pltpu.VMEM((ROWS + 64, HD), f32)],
         compiler_params=pltpu.CompilerParams(vmem_limit_bytes=ROUTE_LIMIT),
         name="route",
     )(block_table.T, ctx_len[None, :], queries)
+    send, pool_keys, pool_values, out_weight = lax.optimization_barrier(
+        (send, pool_keys, pool_values, out_weight)
+    )
     items = lax.all_to_all(
-        send.reshape(PEERS, HEADS + 1, 2, HD), inst, split_axis=0, concat_axis=0, tiled=True
-    )
-    keys, values = stage(pool_keys, pool_values, name="stage_blocks")
-    out_weight, keys, values = lax.optimization_barrier((out_weight, keys, values))
-    other_weight = lax.ppermute(out_weight, "c", [(0, 1), (1, 0)])
-    items, other_weight = lax.optimization_barrier((items, other_weight))
+        send.reshape(PEERS, HEADS + 1, PER, HD), inst, split_axis=0, concat_axis=0, tiled=True
+    )
+    (keys,), values = stage(pool_keys, name="stage_keys"), pool_values
+    swap = lambda v: lax.ppermute(v, "c", [(0, 1), (1, 0)])
+    other_keys, other_values, other_weight = swap(pool_keys), swap(pool_values), swap(out_weight)
+    pick, by_slot = pl.pallas_call(
+        unpack_kernel,
+        out_shape=(
+            jax.ShapeDtypeStruct((PER * PEERS, HD), bf16),
+            jax.ShapeDtypeStruct((SLOTS, (HEADS + 1) * HD), f32),
+        ),
+        in_specs=[VMEM],
+        out_specs=(VMEM, VMEM),
+        scratch_shapes=[pltpu.VMEM((ROWS + 64, HD), f32)],
+        compiler_params=limit,
+        cost_estimate=pl.CostEstimate(flops=17179869184, bytes_accessed=67108864, transcendentals=0),
+        name="unpack",
+    )(items.reshape(ROWS, HD))
+    pick, by_slot, other_keys, other_values = lax.optimization_barrier(
+        (pick, by_slot, other_keys, other_values)
+    )
     back = pl.pallas_call(
         attend_kernel,
         out_shape=jax.ShapeDtypeStruct((ROWS, HD), bf16),
-        in_specs=[VMEM, VMEM, VMEM],
+        in_specs=[VMEM] * 6,
         out_specs=VMEM,
         scratch_shapes=[
-            pltpu.VMEM((ROWS + 32, HD), f32),
+            pltpu.VMEM((ROWS + 64, HD), f32),
             pltpu.VMEM((SLOTS * HEADS + 16, HD), f32),
             pltpu.VMEM((SLOTS * HEADS + 16, HD), f32),
         ],
         compiler_params=limit,
         name="attend",
-    )(items.reshape(ROWS, HD), keys, values)
+    )(pick, by_slot, keys, values, other_keys, other_values)
     partials = lax.all_to_all(
-        back.reshape(PEERS, HEADS + 1, 2, HD), inst, split_axis=0, concat_axis=0, tiled=True
+        back.reshape(PEERS, HEADS + 1, PER, HD), inst, split_axis=0, concat_axis=0, tiled=True
     )
     attention = pl.pallas_call(
         merge_kernel,
         out_shape=jax.ShapeDtypeStruct((32 * REQS, HEADS * HD), bf16),
         in_specs=[VMEM, VMEM],
         out_specs=VMEM,
-        scratch_shapes=[pltpu.VMEM((ROWS + 32, HD), f32)],
+        scratch_shapes=[pltpu.VMEM((ROWS + 64, HD), f32)],
         compiler_params=limit,
         name="merge",
     )(where_to, partials.reshape(ROWS, HD))

time: 87.7 us -> 86 us (0.981)
  blocking collectives: 54.9 us -> 35 us
  starting transfers between devices: 17.2 us -> 28.3 us
  waiting for transfers between devices: 6.92 us -> 14 us
  Pallas kernels: 4.8 us -> 5.99 us
  local copies, waits for them, and re-layouts: 3.16 us -> 2.12 us
    all_to_all x2 -> x1, blocking collectives: 37.4 us -> 15.4 us  [per_device(): lax.all_to_all(back.reshape(PEERS, HEADS + 1, PER, HD), inst, split_axis=...]
    all_to_all x1 -> x2, waiting for transfers between devices: 5.76 us -> 12.8 us  [the longest x1 6.91 us: per_device(): lax.all_to_all(attention.reshape(32, REQS, HEADS * HD), ('x', 'z'), split...]
    ppermute x1 -> x3, starting transfers between devices: 2.25 us -> 9.11 us  [per_device(): swap = lambda v: lax.ppermute(v, 'c', [(0, 1), (1, 0)])]
    all_to_all x1 -> x2, starting transfers between devices: 14.9 us -> 19.2 us  [the longest x1 13.7 us: per_device(): lax.all_to_all(send.reshape(PEERS, HEADS + 1, PER, HD), inst, split_axis=...]
    all_to_all x1, blocking collectives: 17.5 us -> 19.6 us  [per_device(): lax.all_to_all(parts.reshape(16, 32, HD), ('c', 'tp'), split_axis=0, conc...]
    unnamed x8, local copies, waits for them, and re-layouts: 3.16 us -> 2.12 us
  transfers between devices with their start and end apart: 2 -> 5, of which waited for: 2 -> 3; matrix products, arithmetic and copies ran while one was open for 0% -> 0% of each run, Pallas kernels for 0% -> 0%
where the time goes in v7:
time: 86 us; the launch traced here: 85.4 us
  blocking collectives  35 us (41%)
  starting transfers between devices  28.3 us (33%)
  waiting for transfers between devices  14 us (16%)
  Pallas kernels  5.99 us (7%)
  local copies, waits for them, and re-layouts  2.12 us (2%)
    all_to_all x1, blocking collectives, per_device(): lax.all_to_all(parts.reshape(16, 32, HD), ('c', 'tp'), split_axis=0, conc...  19.6 us
    all_to_all x1, blocking collectives, per_device(): lax.all_to_all(back.reshape(PEERS, HEADS + 1, PER, HD), inst, split_axis=...  15.4 us
    all_to_all x1, starting transfers between devices, per_device(): lax.all_to_all(send.reshape(PEERS, HEADS + 1, PER, HD), inst, split_axis=...  13.7 us
    ppermute x3, starting transfers between devices, per_device(): swap = lambda v: lax.ppermute(v, 'c', [(0, 1), (1, 0)])  9.11 us
    all_to_all x1, waiting for transfers between devices, per_device(): lax.all_to_all(attention.reshape(32, REQS, HEADS * HD), ('x', 'z'), split...  6.91 us
    all_to_all x1, waiting for transfers between devices, per_device(): lax.all_to_all(send.reshape(PEERS, HEADS + 1, PER, HD), inst, split_axis=...  5.89 us
    all_to_all x1, starting transfers between devices, per_device(): lax.all_to_all(attention.reshape(32, REQS, HEADS * HD), ('x', 'z'), split...  5.44 us
    unnamed x8, local copies, waits for them, and re-layouts  2.12 us
  transfers between devices with their start and end apart: 5, of which 3 were waited for; matrix products, arithmetic and copies ran while one was open for 0% of the time, Pallas kernels for 0%

profile of v7, /device:TPU:1, one launch (start us, length us, event | category | flops | bytes accessed | tf_op | source)
XLA Modules:
  0.0 85.4 jit_solution(503021899502741972)
XLA Ops:
  0.0 1.9 %route.1 = (bf16[1152,128]{1,0:T(8,128)(2,1)}, bf16[32,128]{1,0:T(8,128)(2,1)}) custom-call(s32[4,8]{1,0:T(4,128)} %bitcast.17, s32[1,8]{1,0:T(1,128)} %bitcast.18, bf16[8,1024]{1,0:T(8,128)(2,1)} %q.1), custom_call_target="tpu_custom_call" | custom-call | tf_op jit(solution)/shard_map/route/pallas_call | solution.py:217
  1.9 13.7 %all-to-all-start = ((bf16[32,9,4,128]{3,2,1,0:T(4,128)(2,1)}), bf16[32,9,4,128]{3,2,1,0:T(4,128)(2,1)S(1)}, u32[]{:S(2)}, u32[]{:S(2)}) async-start(bf16[32,9,4,128]{3,2,1,0:T(4,128)(2,1)} %bitcast.16), calls=%async_computation | async-start | bytes 589824 | tf_op jit(solution)/shard_map/all_to_all | solution.py:232
  15.7 2.9 %collective-permute-start = (bf16[32,128,128]{2,1,0:T(8,128)(2,1)}, bf16[32,128,128]{2,1,0:T(8,128)(2,1)S(1)}, u32[]{:S(2)}, u32[]{:S(2)}) collective-permute-start(bf16[32,128,128]{2,1,0:T(8,128)(2,1)} %refs_0_), channel_id=1, source_target_pairs={{0,8},{8,0},{1,9},{9,1},{2,10},{10,2},{3,11},{11,3},{4,12},{12,4},... | collective-permute-start | bytes 3145736 | tf_op jit(solution)/shard_map/ppermute | solution.py:236
  18.5 1.9 %collective-permute-start.1 = (bf16[32,128,128]{2,1,0:T(8,128)(2,1)}, bf16[32,128,128]{2,1,0:T(8,128)(2,1)S(1)}, u32[]{:S(2)}, u32[]{:S(2)}) collective-permute-start(bf16[32,128,128]{2,1,0:T(8,128)(2,1)} %values), channel_id=1, source_target_pairs={{0,8},{8,0},{1,9},{9,1},{2,10},{10,2},{3,11},{11,3},{4,12},{12,4},... | collective-permute-start | bytes 3145736 | tf_op jit(solution)/shard_map/ppermute | solution.py:236
  20.5 0.0 copy-start
  20.5 1.2 %copy-done = bf16[32,128,128]{2,1,0:T(8,128)(2,1)S(1)} copy-done((bf16[32,128,128]{2,1,0:T(8,128)(2,1)S(1)}, bf16[32,128,128]{2,1,0:T(8,128)(2,1)}, u32[]{:S(2)}) %copy-start) | copy-done | bytes 1048600
  21.7 0.1 stage_keys.1.keys
  21.8 5.9 %all-to-all-done = bf16[32,9,4,128]{3,2,1,0:T(4,128)(2,1)S(1)} async-done(((bf16[32,9,4,128]{3,2,1,0:T(4,128)(2,1)}), bf16[32,9,4,128]{3,2,1,0:T(4,128)(2,1)S(1)}, u32[]{:S(2)}, u32[]{:S(2)}) %all-to-all-start) | async-done | bytes 294944 | tf_op jit(solution)/shard_map/all_to_all | solution.py:232
  27.7 0.0 copy-start.1
  27.7 0.3 unpack.1
  28.0 0.0 collective-permute-done.other_keys
  28.0 0.0 collective-permute-done.1.other_values
  28.0 0.9 %copy-done.1 = bf16[32,128,128]{2,1,0:T(8,128)(2,1)S(1)} copy-done((bf16[32,128,128]{2,1,0:T(8,128)(2,1)S(1)}, bf16[32,128,128]{2,1,0:T(8,128)(2,1)}, u32[]{:S(2)}) %copy-start.1) | copy-done | bytes 1048600
  28.9 0.0 copy-start.3
  28.9 1.3 %attend.1 = bf16[1152,128]{1,0:T(8,128)(2,1)S(1)} custom-call(bf16[128,128]{1,0:T(8,128)(2,1)S(1)} %get-tuple-element.24.pick, f32[64,1152]{1,0:T(8,128)S(1)} %get-tuple-element.25.by_slot, bf16[32,128,128]{2,1,0:T(8,128)(2,1)S(1)} %stage_keys.1.keys, bf16[32,128,128]{2,1,0:T(8,128)(2,1)S(1)} %copy-done.1, ...), custom_call_target="tpu_custom_call" | custom-call | tf_op jit(solution)/shard_map/attend/pallas_call | solution.py:254
  30.3 15.4 %all_to_all.20 = bf16[32,9,4,128]{3,2,1,0:T(4,128)(2,1)S(1)} all-to-all(bf16[32,9,4,128]{3,2,1,0:T(4,128)(2,1)S(1)} %bitcast.11), channel_id=1, replica_groups=mesh['z'=8,'x'=4,'c'=2,'tp'=8] {'z','x'}, dimensions={0} | all-to-all | bytes 589824 | tf_op jit(solution)/shard_map/all_to_all | solution.py:267
  45.7 0.0 copy-done.3
  45.7 1.3 %merge.1 = bf16[256,1024]{1,0:T(8,128)(2,1)} custom-call(bf16[32,128]{1,0:T(8,128)(2,1)S(1)} %copy-done.3, bf16[1152,128]{1,0:T(8,128)(2,1)S(1)} %bitcast.12), custom_call_target="tpu_custom_call" | custom-call | tf_op jit(solution)/shard_map/merge/pallas_call | solution.py:270
  46.9 0.0 copy-start.2
  46.9 5.4 %all-to-all-start.2 = ((bf16[32,8,1024]{2,1,0:T(8,128)(2,1)}), bf16[32,8,1024]{2,1,0:T(8,128)(2,1)S(1)}, u32[]{:S(2)}, u32[]{:S(2)}) async-start(bf16[32,8,1024]{2,1,0:T(8,128)(2,1)} %bitcast.6), calls=%async_computation.2 | async-start | bytes 1048576 | tf_op jit(solution)/shard_map/all_to_all | solution.py:279
  52.4 0.0 copy-done.2
  52.4 4.3 %collective-permute-start.2 = (bf16[1024,128]{1,0:T(8,128)(2,1)S(1)}, bf16[1024,128]{1,0:T(8,128)(2,1)S(1)}, u32[]{:S(2)}, u32[]{:S(2)}) collective-permute-start(bf16[1024,128]{1,0:T(8,128)(2,1)S(1)} %copy-done.2), channel_id=1, source_target_pairs={{0,8},{8,0},{1,9},{9,1},{2,10},{10,2},{3,11},{11,3},{4,12},{12,4},... | collective-permute-start | bytes 786440 | tf_op jit(solution)/shard_map/ppermute | solution.py:236
  56.7 1.1 %collective-permute-done.2.other = bf16[1024,128]{1,0:T(8,128)(2,1)S(1)} collective-permute-done((bf16[1024,128]{1,0:T(8,128)(2,1)S(1)}, bf16[1024,128]{1,0:T(8,128)(2,1)S(1)}, u32[]{:S(2)}, u32[]{:S(2)}) %collective-permute-start.2) | collective-permute-done | bytes 262176 | tf_op jit(solution)/shard_map/ppermute | solution.py:236
  57.8 6.9 %all-to-all-done.2 = bf16[32,8,1024]{2,1,0:T(8,128)(2,1)S(1)} async-done(((bf16[32,8,1024]{2,1,0:T(8,128)(2,1)}), bf16[32,8,1024]{2,1,0:T(8,128)(2,1)S(1)}, u32[]{:S(2)}, u32[]{:S(2)}) %all-to-all-start.2) | async-done | bytes 524320 | tf_op jit(solution)/shard_map/all_to_all | solution.py:279
  64.8 0.4 project.1
  65.2 19.6 %all_to_all.21 = bf16[16,32,128]{2,1,0:T(8,128)(2,1)S(1)} all-to-all(bf16[16,32,128]{2,1,0:T(8,128)(2,1)S(1)} %bitcast.13), channel_id=1, replica_groups=mesh['z'=8,'x'=4,'c'=2,'tp'=8] {'c','tp'}, dimensions={0} | all-to-all | bytes 262144 | tf_op jit(solution)/shard_map/all_to_all | solution.py:290
  84.8 0.6 total.1
Async XLA Ops:
  1.9 25.8 %all-to-all-start = ((bf16[32,9,4,128]{3,2,1,0:T(4,128)(2,1)}), bf16[32,9,4,128]{3,2,1,0:T(4,128)(2,1)S(1)}, u32[]{:S(2)}, u32[]{:S(2)}) async-start(bf16[32,9,4,128]{3,2,1,0:T(4,128)(2,1)} %bitcast.16), calls=%async_computation | async-start | bytes 589824 | tf_op jit(solution)/shard_map/all_to_all | solution.py:232
  15.7 12.4 %collective-permute-start = (bf16[32,128,128]{2,1,0:T(8,128)(2,1)}, bf16[32,128,128]{2,1,0:T(8,128)(2,1)S(1)}, u32[]{:S(2)}, u32[]{:S(2)}) collective-permute-start(bf16[32,128,128]{2,1,0:T(8,128)(2,1)} %refs_0_), channel_id=1, source_target_pairs={{0,8},{8,0},{1,9},{9,1},{2,10},{10,2},{3,11},{11,3},{4,12},{12,4},... | collective-permute-start | bytes 3145736 | tf_op jit(solution)/shard_map/ppermute | solution.py:236
  18.5 9.5 %collective-permute-start.1 = (bf16[32,128,128]{2,1,0:T(8,128)(2,1)}, bf16[32,128,128]{2,1,0:T(8,128)(2,1)S(1)}, u32[]{:S(2)}, u32[]{:S(2)}) collective-permute-start(bf16[32,128,128]{2,1,0:T(8,128)(2,1)} %values), channel_id=1, source_target_pairs={{0,8},{8,0},{1,9},{9,1},{2,10},{10,2},{3,11},{11,3},{4,12},{12,4},... | collective-permute-start | bytes 3145736 | tf_op jit(solution)/shard_map/ppermute | solution.py:236
  20.5 1.2 %copy-start = (bf16[32,128,128]{2,1,0:T(8,128)(2,1)S(1)}, bf16[32,128,128]{2,1,0:T(8,128)(2,1)}, u32[]{:S(2)}) copy-start(bf16[32,128,128]{2,1,0:T(8,128)(2,1)} %refs_0_) | copy-start | bytes 3145732
  27.7 1.2 %copy-start.1 = (bf16[32,128,128]{2,1,0:T(8,128)(2,1)S(1)}, bf16[32,128,128]{2,1,0:T(8,128)(2,1)}, u32[]{:S(2)}) copy-start(bf16[32,128,128]{2,1,0:T(8,128)(2,1)} %values) | copy-start | bytes 3145732
  28.9 16.7 %copy-start.3 = (bf16[32,128]{1,0:T(8,128)(2,1)S(1)}, bf16[32,128]{1,0:T(8,128)(2,1)}, u32[]{:S(2)}) copy-start(bf16[32,128]{1,0:T(8,128)(2,1)} %get-tuple-element.17.where_to) | copy-start | bytes 24580
  46.9 5.5 %copy-start.2 = (bf16[1024,128]{1,0:T(8,128)(2,1)S(1)}, bf16[1024,128]{1,0:T(8,128)(2,1)}, u32[]{:S(2)}) copy-start(bf16[1024,128]{1,0:T(8,128)(2,1)} %own) | copy-start | bytes 786436
  46.9 17.8 %all-to-all-start.2 = ((bf16[32,8,1024]{2,1,0:T(8,128)(2,1)}), bf16[32,8,1024]{2,1,0:T(8,128)(2,1)S(1)}, u32[]{:S(2)}, u32[]{:S(2)}) async-start(bf16[32,8,1024]{2,1,0:T(8,128)(2,1)} %bitcast.6), calls=%async_computation.2 | async-start | bytes 1048576 | tf_op jit(solution)/shard_map/all_to_all | solution.py:279
  52.4 5.5 %collective-permute-start.2 = (bf16[1024,128]{1,0:T(8,128)(2,1)S(1)}, bf16[1024,128]{1,0:T(8,128)(2,1)S(1)}, u32[]{:S(2)}, u32[]{:S(2)}) collective-permute-start(bf16[1024,128]{1,0:T(8,128)(2,1)S(1)} %copy-done.2), channel_id=1, source_target_pairs={{0,8},{8,0},{1,9},{9,1},{2,10},{10,2},{3,11},{11,3},{4,12},{12,4},... | collective-permute-start | bytes 786440 | tf_op jit(solution)/shard_map/ppermute | solution.py:236

commit v8 on v7

--- a/solution.py
+++ b/solution.py
@@ -63,7 +63,7 @@
     holders = jnp.sum(jnp.where(row == lane, holder, 0.0), axis=0, keepdims=True)
     earlier = jnp.where((holder == holders) & (lane < row), 1.0, 0.0)
     away = (inst & 1) ^ lax.axis_index("c")
-    place = (away * 2 * PEERS + (inst >> 1)).astype(f32)
+    place = (away * 2 * PEERS + ((inst >> 1) & 3) * 8 + (inst >> 3)).astype(f32)
     item = jnp.sum(earlier, axis=1, keepdims=True) * PEERS + place
     pick = jnp.where(lane.astype(f32) == item, 1.0, 0.0).astype(bf16)
     where_to[...] = pick
@@ -213,7 +213,7 @@
 
 
 def per_device(queries, pool_keys, pool_values, block_table, ctx_len, out_weight):
-    inst = ("z", "x")
+    inst = ("x", "z")
     send, where_to = pl.pallas_call(
         route_kernel,
         out_shape=(

time: 86 us -> 86 us (level)
  waiting for transfers between devices: 14 us -> 12.2 us
  starting transfers between devices: 28.3 us -> 29.3 us
    all_to_all x1, waiting for transfers between devices: 5.89 us -> 3.79 us  [per_device(): lax.all_to_all(send.reshape(PEERS, HEADS + 1, PER, HD), inst, split_axis=...]
    all_to_all x1, starting transfers between devices: 5.44 us -> 6.53 us  [per_device(): lax.all_to_all(attention.reshape(32, REQS, HEADS * HD), ('x', 'z'), split...]
    all_to_all x1, blocking collectives: 15.4 us -> 16.3 us  [per_device(): lax.all_to_all(back.reshape(PEERS, HEADS + 1, PER, HD), inst, split_axis=...]
where the time goes in v8:
time: 86 us; the launch traced here: 85.4 us
  blocking collectives  35.7 us (42%)
  starting transfers between devices  29.3 us (34%)
  waiting for transfers between devices  12.2 us (14%)
  Pallas kernels  5.99 us (7%)
  local copies, waits for them, and re-layouts  2.12 us (2%)
    all_to_all x1, blocking collectives, per_device(): lax.all_to_all(parts.reshape(16, 32, HD), ('c', 'tp'), split_axis=0, conc...  19.4 us
    all_to_all x1, blocking collectives, per_device(): lax.all_to_all(back.reshape(PEERS, HEADS + 1, PER, HD), inst, split_axis=...  16.3 us
    all_to_all x1, starting transfers between devices, per_device(): lax.all_to_all(send.reshape(PEERS, HEADS + 1, PER, HD), inst, split_axis=...  13.7 us
    ppermute x3, starting transfers between devices, per_device(): swap = lambda v: lax.ppermute(v, 'c', [(0, 1), (1, 0)])  9.02 us
    all_to_all x1, waiting for transfers between devices, per_device(): lax.all_to_all(attention.reshape(32, REQS, HEADS * HD), ('x', 'z'), split...  7.3 us
    all_to_all x1, starting transfers between devices, per_device(): lax.all_to_all(attention.reshape(32, REQS, HEADS * HD), ('x', 'z'), split...  6.53 us
    all_to_all x1, waiting for transfers between devices, per_device(): lax.all_to_all(send.reshape(PEERS, HEADS + 1, PER, HD), inst, split_axis=...  3.79 us
    unnamed x8, local copies, waits for them, and re-layouts  2.12 us
  transfers between devices with their start and end apart: 5, of which 3 were waited for; matrix products, arithmetic and copies ran while one was open for 0% of the time, Pallas kernels for 0%

profile of v8, /device:TPU:1, one launch (start us, length us, event | category | flops | bytes accessed | tf_op | source)
XLA Modules:
  0.0 85.4 jit_solution(3103065464565176838)
XLA Ops:
  0.0 1.9 %route.1 = (bf16[1152,128]{1,0:T(8,128)(2,1)}, bf16[32,128]{1,0:T(8,128)(2,1)}) custom-call(s32[4,8]{1,0:T(4,128)} %bitcast.17, s32[1,8]{1,0:T(1,128)} %bitcast.18, bf16[8,1024]{1,0:T(8,128)(2,1)} %q.1), custom_call_target="tpu_custom_call" | custom-call | tf_op jit(solution)/shard_map/route/pallas_call | solution.py:217
  1.9 13.7 %all-to-all-start = ((bf16[32,9,4,128]{3,2,1,0:T(4,128)(2,1)}), bf16[32,9,4,128]{3,2,1,0:T(4,128)(2,1)S(1)}, u32[]{:S(2)}, u32[]{:S(2)}) async-start(bf16[32,9,4,128]{3,2,1,0:T(4,128)(2,1)} %bitcast.16), calls=%async_computation | async-start | bytes 589824 | tf_op jit(solution)/shard_map/all_to_all | solution.py:232
  15.7 2.9 %collective-permute-start = (bf16[32,128,128]{2,1,0:T(8,128)(2,1)}, bf16[32,128,128]{2,1,0:T(8,128)(2,1)S(1)}, u32[]{:S(2)}, u32[]{:S(2)}) collective-permute-start(bf16[32,128,128]{2,1,0:T(8,128)(2,1)} %refs_0_), channel_id=1, source_target_pairs={{0,8},{8,0},{1,9},{9,1},{2,10},{10,2},{3,11},{11,3},{4,12},{12,4},... | collective-permute-start | bytes 3145736 | tf_op jit(solution)/shard_map/ppermute | solution.py:236
  18.5 1.9 %collective-permute-start.1 = (bf16[32,128,128]{2,1,0:T(8,128)(2,1)}, bf16[32,128,128]{2,1,0:T(8,128)(2,1)S(1)}, u32[]{:S(2)}, u32[]{:S(2)}) collective-permute-start(bf16[32,128,128]{2,1,0:T(8,128)(2,1)} %values), channel_id=1, source_target_pairs={{0,8},{8,0},{1,9},{9,1},{2,10},{10,2},{3,11},{11,3},{4,12},{12,4},... | collective-permute-start | bytes 3145736 | tf_op jit(solution)/shard_map/ppermute | solution.py:236
  20.5 0.0 copy-start
  20.5 1.2 %copy-done = bf16[32,128,128]{2,1,0:T(8,128)(2,1)S(1)} copy-done((bf16[32,128,128]{2,1,0:T(8,128)(2,1)S(1)}, bf16[32,128,128]{2,1,0:T(8,128)(2,1)}, u32[]{:S(2)}) %copy-start) | copy-done | bytes 1048600
  21.7 0.1 stage_keys.1.keys
  21.8 3.8 %all-to-all-done = bf16[32,9,4,128]{3,2,1,0:T(4,128)(2,1)S(1)} async-done(((bf16[32,9,4,128]{3,2,1,0:T(4,128)(2,1)}), bf16[32,9,4,128]{3,2,1,0:T(4,128)(2,1)S(1)}, u32[]{:S(2)}, u32[]{:S(2)}) %all-to-all-start) | async-done | bytes 294944 | tf_op jit(solution)/shard_map/all_to_all | solution.py:232
  25.6 0.0 copy-start.1
  25.6 0.3 unpack.1
  25.9 0.0 collective-permute-done.other_keys
  25.9 0.0 collective-permute-done.1.other_values
  25.9 0.9 %copy-done.1 = bf16[32,128,128]{2,1,0:T(8,128)(2,1)S(1)} copy-done((bf16[32,128,128]{2,1,0:T(8,128)(2,1)S(1)}, bf16[32,128,128]{2,1,0:T(8,128)(2,1)}, u32[]{:S(2)}) %copy-start.1) | copy-done | bytes 1048600
  26.8 0.0 copy-start.3
  26.8 1.3 %attend.1 = bf16[1152,128]{1,0:T(8,128)(2,1)S(1)} custom-call(bf16[128,128]{1,0:T(8,128)(2,1)S(1)} %get-tuple-element.24.pick, f32[64,1152]{1,0:T(8,128)S(1)} %get-tuple-element.25.by_slot, bf16[32,128,128]{2,1,0:T(8,128)(2,1)S(1)} %stage_keys.1.keys, bf16[32,128,128]{2,1,0:T(8,128)(2,1)S(1)} %copy-done.1, ...), custom_call_target="tpu_custom_call" | custom-call | tf_op jit(solution)/shard_map/attend/pallas_call | solution.py:254
  28.2 16.3 %all_to_all.20 = bf16[32,9,4,128]{3,2,1,0:T(4,128)(2,1)S(1)} all-to-all(bf16[32,9,4,128]{3,2,1,0:T(4,128)(2,1)S(1)} %bitcast.11), channel_id=1, replica_groups=mesh['z'=8,'x'=4,'c'=2,'tp'=8] {'x','z'}, dimensions={0} | all-to-all | bytes 589824 | tf_op jit(solution)/shard_map/all_to_all | solution.py:267
  44.5 0.0 copy-done.3
  44.5 1.3 %merge.1 = bf16[256,1024]{1,0:T(8,128)(2,1)} custom-call(bf16[32,128]{1,0:T(8,128)(2,1)S(1)} %copy-done.3, bf16[1152,128]{1,0:T(8,128)(2,1)S(1)} %bitcast.12), custom_call_target="tpu_custom_call" | custom-call | tf_op jit(solution)/shard_map/merge/pallas_call | solution.py:270
  45.7 0.0 copy-start.2
  45.7 6.5 %all-to-all-start.2 = ((bf16[32,8,1024]{2,1,0:T(8,128)(2,1)}), bf16[32,8,1024]{2,1,0:T(8,128)(2,1)S(1)}, u32[]{:S(2)}, u32[]{:S(2)}) async-start(bf16[32,8,1024]{2,1,0:T(8,128)(2,1)} %bitcast.6), calls=%async_computation.2 | async-start | bytes 1048576 | tf_op jit(solution)/shard_map/all_to_all | solution.py:279
  52.3 0.0 copy-done.2
  52.3 4.2 %collective-permute-start.2 = (bf16[1024,128]{1,0:T(8,128)(2,1)S(1)}, bf16[1024,128]{1,0:T(8,128)(2,1)S(1)}, u32[]{:S(2)}, u32[]{:S(2)}) collective-permute-start(bf16[1024,128]{1,0:T(8,128)(2,1)S(1)} %copy-done.2), channel_id=1, source_target_pairs={{0,8},{8,0},{1,9},{9,1},{2,10},{10,2},{3,11},{11,3},{4,12},{12,4},... | collective-permute-start | bytes 786440 | tf_op jit(solution)/shard_map/ppermute | solution.py:236
  56.5 1.1 %collective-permute-done.2.other = bf16[1024,128]{1,0:T(8,128)(2,1)S(1)} collective-permute-done((bf16[1024,128]{1,0:T(8,128)(2,1)S(1)}, bf16[1024,128]{1,0:T(8,128)(2,1)S(1)}, u32[]{:S(2)}, u32[]{:S(2)}) %collective-permute-start.2) | collective-permute-done | bytes 262176 | tf_op jit(solution)/shard_map/ppermute | solution.py:236
  57.7 7.3 %all-to-all-done.2 = bf16[32,8,1024]{2,1,0:T(8,128)(2,1)S(1)} async-done(((bf16[32,8,1024]{2,1,0:T(8,128)(2,1)}), bf16[32,8,1024]{2,1,0:T(8,128)(2,1)S(1)}, u32[]{:S(2)}, u32[]{:S(2)}) %all-to-all-start.2) | async-done | bytes 524320 | tf_op jit(solution)/shard_map/all_to_all | solution.py:279
  65.0 0.4 project.1
  65.4 19.4 %all_to_all.21 = bf16[16,32,128]{2,1,0:T(8,128)(2,1)S(1)} all-to-all(bf16[16,32,128]{2,1,0:T(8,128)(2,1)S(1)} %bitcast.13), channel_id=1, replica_groups=mesh['z'=8,'x'=4,'c'=2,'tp'=8] {'c','tp'}, dimensions={0} | all-to-all | bytes 262144 | tf_op jit(solution)/shard_map/all_to_all | solution.py:290
  84.8 0.6 total.1
Async XLA Ops:
  1.9 23.7 %all-to-all-start = ((bf16[32,9,4,128]{3,2,1,0:T(4,128)(2,1)}), bf16[32,9,4,128]{3,2,1,0:T(4,128)(2,1)S(1)}, u32[]{:S(2)}, u32[]{:S(2)}) async-start(bf16[32,9,4,128]{3,2,1,0:T(4,128)(2,1)} %bitcast.16), calls=%async_computation | async-start | bytes 589824 | tf_op jit(solution)/shard_map/all_to_all | solution.py:232
  15.7 10.3 %collective-permute-start = (bf16[32,128,128]{2,1,0:T(8,128)(2,1)}, bf16[32,128,128]{2,1,0:T(8,128)(2,1)S(1)}, u32[]{:S(2)}, u32[]{:S(2)}) collective-permute-start(bf16[32,128,128]{2,1,0:T(8,128)(2,1)} %refs_0_), channel_id=1, source_target_pairs={{0,8},{8,0},{1,9},{9,1},{2,10},{10,2},{3,11},{11,3},{4,12},{12,4},... | collective-permute-start | bytes 3145736 | tf_op jit(solution)/shard_map/ppermute | solution.py:236
  18.5 7.4 %collective-permute-start.1 = (bf16[32,128,128]{2,1,0:T(8,128)(2,1)}, bf16[32,128,128]{2,1,0:T(8,128)(2,1)S(1)}, u32[]{:S(2)}, u32[]{:S(2)}) collective-permute-start(bf16[32,128,128]{2,1,0:T(8,128)(2,1)} %values), channel_id=1, source_target_pairs={{0,8},{8,0},{1,9},{9,1},{2,10},{10,2},{3,11},{11,3},{4,12},{12,4},... | collective-permute-start | bytes 3145736 | tf_op jit(solution)/shard_map/ppermute | solution.py:236
  20.5 1.2 %copy-start = (bf16[32,128,128]{2,1,0:T(8,128)(2,1)S(1)}, bf16[32,128,128]{2,1,0:T(8,128)(2,1)}, u32[]{:S(2)}) copy-start(bf16[32,128,128]{2,1,0:T(8,128)(2,1)} %refs_0_) | copy-start | bytes 3145732
  25.6 1.2 %copy-start.1 = (bf16[32,128,128]{2,1,0:T(8,128)(2,1)S(1)}, bf16[32,128,128]{2,1,0:T(8,128)(2,1)}, u32[]{:S(2)}) copy-start(bf16[32,128,128]{2,1,0:T(8,128)(2,1)} %values) | copy-start | bytes 3145732
  26.8 17.6 %copy-start.3 = (bf16[32,128]{1,0:T(8,128)(2,1)S(1)}, bf16[32,128]{1,0:T(8,128)(2,1)}, u32[]{:S(2)}) copy-start(bf16[32,128]{1,0:T(8,128)(2,1)} %get-tuple-element.17.where_to) | copy-start | bytes 24580
  45.7 6.5 %copy-start.2 = (bf16[1024,128]{1,0:T(8,128)(2,1)S(1)}, bf16[1024,128]{1,0:T(8,128)(2,1)}, u32[]{:S(2)}) copy-start(bf16[1024,128]{1,0:T(8,128)(2,1)} %own) | copy-start | bytes 786436
  45.7 19.2 %all-to-all-start.2 = ((bf16[32,8,1024]{2,1,0:T(8,128)(2,1)}), bf16[32,8,1024]{2,1,0:T(8,128)(2,1)S(1)}, u32[]{:S(2)}, u32[]{:S(2)}) async-start(bf16[32,8,1024]{2,1,0:T(8,128)(2,1)} %bitcast.6), calls=%async_computation.2 | async-start | bytes 1048576 | tf_op jit(solution)/shard_map/all_to_all | solution.py:279
  52.3 5.4 %collective-permute-start.2 = (bf16[1024,128]{1,0:T(8,128)(2,1)S(1)}, bf16[1024,128]{1,0:T(8,128)(2,1)S(1)}, u32[]{:S(2)}, u32[]{:S(2)}) collective-permute-start(bf16[1024,128]{1,0:T(8,128)(2,1)S(1)} %copy-done.2), channel_id=1, source_target_pairs={{0,8},{8,0},{1,9},{9,1},{2,10},{10,2},{3,11},{11,3},{4,12},{12,4},... | collective-permute-start | bytes 786440 | tf_op jit(solution)/shard_map/ppermute | solution.py:236
